TPU v7x, 256 devices: a whole 4x4x8 slice. The times are simulated.
256 devices in a mesh: dp: 16 (over z, x_lo), seq: 16 (over y, x_hi, core).
Axes of the slice: x: 4 (x_hi: 2, x_lo: 2; x = x_hi * 2 + x_lo), y: 4, z: 8, core: 2. Of those that a mesh axis runs over, the one named last changes fastest.
Arguments:
- inputs: bfloat16 [16, 2048, 768], P('dp', 'seq'), may hold values from -6 to 6
- convolution_weight: bfloat16 [5, 768, 768], replicated, may hold values from -0.09375 to 0.09375
- w_qkv: bfloat16 [768, 3072], replicated, may hold values from -0.21875 to 0.21875
- gain: float32 [768], replicated, may hold values from 0.5 to 1.5
- out_grad: bfloat16 [16, 2048, 1024], P('dp', 'seq'), may hold values from -6 to 6
Outputs:
- attended: bfloat16 [16, 2048, 1024], P('dp', 'seq')
- grad_input: bfloat16 [16, 2048, 768], P('dp', 'seq')
- grad_conv: float32 [5, 768, 768], P(None, None, 'seq')
- grad_qkv: float32 [768, 3072], P(None, 'seq')
All inputs are finite; a program needn't handle non-finite values.
Results may differ from a plain program's by a relative error of at most 0.023.
Values may be sent and summed in bfloat16 or wider, within the bound.
A program may use at most 128 MiB of HBM per device.

v0:
```python
import jax
import jax.numpy as jnp
from jax import lax
from jax.sharding import PartitionSpec as P

CH = 768
HEADS = 8
HD = 128
KERNEL_TAPS = 5
TAP_SPACING = 16


def with_halo(x, sides, width):
    for axis, dim in sides:
        devices, length = (lax.axis_size(axis), x.shape[dim])
        up = [(i, (i + 1) % devices) for i in range(devices - 1)]
        down = [(j, i) for i, j in up]
        last = lax.slice_in_dim(x, length - width, length, axis=dim)
        initial = lax.slice_in_dim(x, 0, width, axis=dim)
        before = lax.ppermute(last, axis, up)
        after = lax.ppermute(initial, axis, down)
        x = jnp.concatenate([before, x, after], axis=dim)
    return x


def body(inputs, convolution_weight, w_qkv, gain, out_grad):
    local_rows = inputs.shape[1]
    inner = HEADS * HD
    half_reach = KERNEL_TAPS // 2
    temper = HD ** (-0.5)
    tap_place = lax.axis_index("seq")
    local_in = inputs[0].astype(jnp.float32)
    acted, gelu_back = jax.vjp(jax.nn.gelu, local_in)
    activated_low_precision = acted.astype(jnp.bfloat16)
    activated_rows_full = lax.all_gather(activated_low_precision, "seq", axis=0, tiled=True)
    padded_length = activated_rows_full.shape[0]
    padded_rows_full = jnp.pad(
        activated_rows_full, ((half_reach * TAP_SPACING, half_reach * TAP_SPACING), (0, 0))
    )
    tap_window = lax.dynamic_slice_in_dim(
        padded_rows_full, tap_place * local_rows, local_rows + 2 * half_reach * TAP_SPACING, 0
    )
    convolved_output = jnp.zeros((local_rows, CH), jnp.float32)
    for tap_number in range(KERNEL_TAPS):
        convolved_output = convolved_output + jnp.dot(
            tap_window[tap_number * TAP_SPACING : tap_number * TAP_SPACING + local_rows],
            convolution_weight[tap_number],
            preferred_element_type=jnp.float32,
        )
    hidden = local_in + convolved_output
    inv_rms = lax.rsqrt(jnp.mean(hidden * hidden, -1, keepdims=True) + 1e-06)
    normed = hidden * inv_rms
    normed_bf = (normed * gain).astype(jnp.bfloat16)
    normed_all = lax.all_gather(normed_bf, "seq", axis=0, tiled=True)
    query = jnp.dot(normed_bf, w_qkv[:, :inner], preferred_element_type=jnp.float32).astype(
        jnp.bfloat16
    )
    keyval = jnp.dot(normed_all, w_qkv[:, inner:], preferred_element_type=jnp.float32).astype(
        jnp.bfloat16
    )
    query_heads = query.reshape(local_rows, HEADS, HD)
    key_heads = keyval[:, :inner].reshape(padded_length, HEADS, HD)
    value_heads = keyval[:, inner:].reshape(padded_length, HEADS, HD)
    scores = (
        jnp.einsum("qhd,khd->hqk", query_heads, key_heads, preferred_element_type=jnp.float32)
        * temper
    )
    highest = jnp.max(scores, -1, keepdims=True)
    expo = jnp.exp(scores - highest)
    denom = jnp.sum(expo, -1, keepdims=True)
    log_total = highest + jnp.log(denom)
    weights_bf = jnp.exp(scores - log_total).astype(jnp.bfloat16)
    attended = jnp.einsum(
        "hqk,khd->qhd", weights_bf, value_heads, preferred_element_type=jnp.float32
    ).astype(jnp.bfloat16)
    grad_heads = out_grad[0].reshape(local_rows, HEADS, HD)
    back_weights = jnp.exp(scores - log_total)
    grad_weights = jnp.einsum(
        "qhd,khd->hqk", grad_heads, value_heads, preferred_element_type=jnp.float32
    )
    row_dots = jnp.sum(grad_heads.astype(jnp.float32) * attended.astype(jnp.float32), -1)
    grad_scores = (back_weights * (grad_weights - row_dots.T[..., None])).astype(jnp.bfloat16)
    grad_query = (
        jnp.einsum("hqk,khd->qhd", grad_scores, key_heads, preferred_element_type=jnp.float32)
        * temper
    ).astype(jnp.bfloat16)
    query_all, grad_all = (
        lax.all_gather(query_heads, "seq", axis=0, tiled=True),
        lax.all_gather(grad_heads, "seq", axis=0, tiled=True),
    )
    totals_all, dots_all = (
        lax.all_gather(log_total[..., 0].T, "seq", axis=0, tiled=True),
        lax.all_gather(row_dots, "seq", axis=0, tiled=True),
    )
    own_keys = lax.dynamic_slice_in_dim(key_heads, tap_place * local_rows, local_rows, 0)
    own_values = lax.dynamic_slice_in_dim(value_heads, tap_place * local_rows, local_rows, 0)
    far_scores = (
        jnp.einsum("qhd,khd->hqk", query_all, own_keys, preferred_element_type=jnp.float32) * temper
    )
    far_weights = jnp.exp(far_scores - totals_all.T[..., None])
    far_grad = jnp.einsum("qhd,khd->hqk", grad_all, own_values, preferred_element_type=jnp.float32)
    far_scores_bf = (far_weights * (far_grad - dots_all.T[..., None])).astype(jnp.bfloat16)
    grad_key = (
        jnp.einsum("hqk,qhd->khd", far_scores_bf, query_all, preferred_element_type=jnp.float32)
        * temper
    ).astype(jnp.bfloat16)
    grad_value = jnp.einsum(
        "hqk,qhd->khd",
        far_weights.astype(jnp.bfloat16),
        grad_all,
        preferred_element_type=jnp.float32,
    ).astype(jnp.bfloat16)
    grad_key = grad_key.reshape(local_rows, inner)
    grad_value = grad_value.reshape(local_rows, inner)
    grad_rows = jnp.concatenate([grad_query.reshape(local_rows, inner), grad_key, grad_value], 1)
    grad_normed = lax.dot_general(
        grad_rows, w_qkv, (((1,), (1,)), ((), ())), preferred_element_type=jnp.float32
    )
    scaled = grad_normed * gain
    grad_hidden = inv_rms * (scaled - normed * jnp.mean(scaled * normed, -1, keepdims=True))
    convolved_output_gradient = grad_hidden.astype(jnp.bfloat16)
    border_rows = with_halo(convolved_output_gradient, (("seq", 0),), half_reach * TAP_SPACING)
    grad_acted = jnp.zeros((local_rows, CH), jnp.float32)
    for tap_number in range(KERNEL_TAPS):
        tap_offset = (KERNEL_TAPS - 1 - tap_number) * TAP_SPACING
        grad_acted = grad_acted + lax.dot_general(
            border_rows[tap_offset : tap_offset + local_rows],
            convolution_weight[tap_number],
            (((1,), (1,)), ((), ())),
            preferred_element_type=jnp.float32,
        )
    grad_input = (grad_hidden + gelu_back(grad_acted)[0]).astype(jnp.bfloat16)
    cols_qkv, cols_conv = (
        lax.all_to_all(grad_rows, "seq", split_axis=1, concat_axis=0, tiled=True),
        lax.all_to_all(convolved_output_gradient, "seq", split_axis=1, concat_axis=0, tiled=True),
    )
    qkv_part = lax.dot_general(
        normed_all, cols_qkv, (((0,), (0,)), ((), ())), preferred_element_type=jnp.float32
    )
    convolved_partial = jnp.stack(
        [
            lax.dot_general(
                padded_rows_full[
                    tap_number * TAP_SPACING : tap_number * TAP_SPACING + padded_length
                ],
                cols_conv,
                (((0,), (0,)), ((), ())),
                preferred_element_type=jnp.float32,
            )
            for tap_number in range(KERNEL_TAPS)
        ],
        0,
    )
    conv_sum, qkv_sum = (
        lax.psum(convolved_partial.astype(jnp.bfloat16), "dp").astype(jnp.float32),
        lax.psum(qkv_part.astype(jnp.bfloat16), "dp").astype(jnp.float32),
    )
    return (attended.reshape(1, local_rows, inner), grad_input[None], conv_sum, qkv_sum)


def solution(mesh):
    in_specs = (P("dp", "seq", None), P(), P(), P(), P("dp", "seq", None))
    out_specs = (P("dp", "seq", None), P("dp", "seq", None), P(None, None, "seq"), P(None, "seq"))
    return jax.shard_map(body, mesh=mesh, in_specs=in_specs, out_specs=out_specs, check_vma=False)
```

profile of v0, /device:TPU:6, one launch (start us, length us, event | category | flops | bytes accessed | tf_op | source)
XLA Modules:
  0.0 471.3 jit_solution(6670505479542289030)
XLA Ops:
  9.0 59.5 %all-gather.5.cloned.1.call-done = bf16[2048,768]{1,0:T(8,128)(2,1)} async-done(((bf16[128,768]{1,0:T(8,128)(2,1)}), bf16[2048,768]{1,0:T(8,128)(2,1)}) %all-gather.5.cloned.1.call-update) | async-done | bytes 3145744 | tf_op jit(solution)/shard_map/all_gather | solution.py:35
  68.5 1.8 fusion.53
  70.8 2.3 convolution_add_fusion.5
  75.5 1.9 fusion.55
  78.9 1.8 copy.27
  80.7 49.5 %all-gather.7.cloned.1.call-done = bf16[2048,768]{1,0:T(8,128)(2,1)} async-done(((bf16[128,768]{1,0:T(8,128)(2,1)}), bf16[2048,768]{1,0:T(8,128)(2,1)}) %all-gather.7.cloned.1.call-update) | async-done | bytes 3145744 | tf_op jit(solution)/shard_map/all_gather | solution.py:54
  130.2 9.3 %convolution_convert_fusion = bf16[2048,2048]{0,1:T(8,128)(2,1)S(1)} fusion(bf16[2048,768]{1,0:T(8,128)(2,1)} %all-gather.7.cloned.1.call-done, bf16[768,3072]{1,0:T(8,128)(2,1)} %param.7), kind=kOutput, calls=%fused_computation.7 | convolution fusion | flops 6446645248 | bytes 14680064 | tf_op jit(solution)/shard_map/dot_general | solution.py:58
  144.2 2.2 copy-done
  146.4 2.7 multiply_reduce_fusion.1
  150.9 22.6 %all_gather.23 = f32[2048,8]{0,1:T(8,128)} all-gather(f32[128,8]{0,1:T(8,128)S(1)} %get-tuple-element.26), channel_id=1, replica_groups=mesh['dp'=16,'seq'=16] {'seq'}, dimensions={0}, use_global_device_ids=true | all-gather | bytes 69632 | tf_op jit(solution)/shard_map/all_gather | solution.py:93
  173.5 24.3 %all_gather.21 = f32[2048,8]{0,1:T(8,128)} all-gather(f32[128,8]{0,1:T(8,128)S(1)} %bitcast.180), channel_id=1, replica_groups=mesh['dp'=16,'seq'=16] {'seq'}, dimensions={0}, use_global_device_ids=true | all-gather | bytes 69632 | tf_op jit(solution)/shard_map/all_gather | solution.py:92
  197.8 10.2 %fusion.27 = bf16[8,128,128]{2,1,0:T(8,128)(2,1)} fusion(bf16[2048,8,128]{0,2,1:T(8,128)(2,1)} %bitcast.160, f32[8,128,2048]{2,1,0:T(8,128)} %copy-done, bf16[2048,8,128]{0,2,1:T(8,128)(2,1)} %bitcast.163, bf16[128,8,128]{0,2,1:T(8,128)(2,1)} %bitcast.167, f32[8,128]{1,0:T(8,128)S(1)} %bitcast.181, f32[8,128]{1,0:T(8,128)S(1)} %log_add_fusion), kind=kOutput, calls=%fused_computation.33 | convolution fusion | flops 1084489728 | bytes 17309696 | tf_op jit(solution)/shard_map/hqk,khd->qhd/dot_general | solution.py:84
  207.9 6.8 %fusion.130 = f32[8,2048,128]{2,1,0:T(8,128)} fusion(bf16[2048,8,128]{2,0,1:T(8,128)(2,1)} %all-gather.9.cloned.1.call-done, bf16[2048,8,128]{0,2,1:T(8,128)(2,1)} %bitcast.161, s32[]{:T(128)S(6)} %select_n.8), kind=kOutput, calls=%fused_computation.124 | convolution fusion | flops 536870912 | bytes 12845060 | tf_op jit(solution)/shard_map/qhd,khd->hqk/dot_general | solution.py:98
  214.7 40.5 %all-gather.11.cloned.1.call-done = bf16[2048,8,128]{0,2,1:T(8,128)(2,1)} async-done(((bf16[128,8,128]{0,2,1:T(8,128)(2,1)}), bf16[2048,8,128]{0,2,1:T(8,128)(2,1)}) %all-gather.11.cloned.1.call-update) | async-done | bytes 4194320 | tf_op jit(solution)/shard_map/all_gather | solution.py:89
  255.2 6.8 %fusion.35 = bf16[8,128,128]{1,2,0:T(8,128)(2,1)} fusion(bf16[2048,8,128]{0,2,1:T(8,128)(2,1)} %all-gather.11.cloned.1.call-done, f32[8,2048,128]{2,1,0:T(8,128)} %fusion.130, f32[8,2048]{1,0:T(8,128)} %bitcast.173), kind=kOutput, calls=%fused_computation.37 | convolution fusion | flops 543293440 | bytes 12910592 | tf_op jit(solution)/shard_map/hqk,qhd->khd/dot_general | solution.py:107
  262.0 11.3 %fusion.28 = bf16[8,128,128]{2,1,0:T(8,128)(2,1)} fusion(bf16[2048,8,128]{2,0,1:T(8,128)(2,1)} %all-gather.9.cloned.1.call-done, f32[8,2048,128]{2,1,0:T(8,128)} %fusion.130, bf16[2048,8,128]{0,2,1:T(8,128)(2,1)} %all-gather.11.cloned.1.call-done, f32[8,2048]{1,0:T(8,128)} %bitcast.179, f32[8,2048]{1,0:T(8,128)} %bitcast.174, ...), kind=kOutput, calls=%fused_computation.34 | convolution fusion | flops 1084489728 | bytes 17432580 | tf_op jit(solution)/shard_map/hqk,qhd->khd/dot_general | solution.py:104
  273.3 2.1 pad_maximum_fusion
  275.3 4.4 multiply_reduce_fusion.2
  282.3 3.8 collective-permute-start
  286.1 2.6 fusion.46
  289.5 5.6 %all-to-all-start = ((bf16[128,16,48]{0,2,1:T(8,128)(2,1)}), bf16[128,16,48]{0,2,1:T(8,128)(2,1)S(1)}, u32[]{:S(2)}, u32[]{:S(2)}) async-start(bf16[128,16,48]{0,2,1:T(8,128)(2,1)} %bitcast.25), calls=%async_computation | async-start | bytes 393216 | tf_op jit(solution)/shard_map/all_to_all | solution.py:135
  295.1 2.3 collective-permute-start.1
  297.4 2.6 fusion.49
  300.9 7.2 %all-to-all-start.1 = ((bf16[128,16,192]{0,2,1:T(8,128)(2,1)}), bf16[128,16,192]{0,2,1:T(8,128)(2,1)}, u32[]{:S(2)}, u32[]{:S(2)}) async-start(bf16[128,16,192]{0,2,1:T(8,128)(2,1)} %bitcast.165), calls=%async_computation.1 | async-start | bytes 1572864 | tf_op jit(solution)/shard_map/all_to_all | solution.py:134
  314.6 6.2 %all-to-all-done.1 = bf16[128,16,192]{0,2,1:T(8,128)(2,1)} async-done(((bf16[128,16,192]{0,2,1:T(8,128)(2,1)}), bf16[128,16,192]{0,2,1:T(8,128)(2,1)}, u32[]{:S(2)}, u32[]{:S(2)}) %all-to-all-start.1) | async-done | bytes 786464 | tf_op jit(solution)/shard_map/all_to_all | solution.py:134
  320.8 3.6 convolution_convert_fusion.1
  324.5 1.8 fusion.41
  326.3 1.8 fusion.39
  328.2 2.6 fusion.125
  330.8 130.2 %all-reduce.4.cloned.1.call-done = (bf16[5,768,48]{1,2,0:T(8,128)(2,1)}, bf16[768,192]{0,1:T(8,128)(2,1)}) async-done(((bf16[5,768,48]{1,2,0:T(8,128)(2,1)}, bf16[768,192]{0,1:T(8,128)(2,1)}), (bf16[5,768,48]{1,2,0:T(8,128)(2,1)}, bf16[768,192]{0,1:T(8,128)(2,1)})) %all-reduce.4.cloned.1.call-update) | async-done | bytes 663568 | tf_op jit(solution)/shard_map/psum | solution.py:155
  461.1 1.9 convert_element_type.100
  463.0 1.8 convert_element_type.102
  (68 shorter events, 23.3 us)
Async XLA Ops:
  7.2 61.3 %all-gather.5.cloned.1.call-start = ((), (), s32[]{:S(2)}) async-start(), calls=%async_computation.2 | async-start | bytes 3342336 | tf_op jit(solution)/shard_map/all_gather | solution.py:35
  9.0 121.2 %all-gather.7.cloned.1.call-start = ((), (), s32[]{:S(2)}) async-start(), calls=%async_computation.3 | async-start | bytes 3342336 | tf_op jit(solution)/shard_map/all_gather | solution.py:54
  68.5 2.3 copy-start.1
  68.5 4.7 copy-start.4
  73.2 0.9 copy-start.11
  73.5 1.0 copy-start.16
  74.5 200.8 %copy-start.5 = (f32[128,768]{1,0:T(8,128)}, f32[128,768]{1,0:T(8,128)S(1)}, u32[]{:S(2)}) copy-start(f32[128,768]{1,0:T(8,128)S(1)} %get-tuple-element.23) | copy-start | bytes 1179652
  75.4 132.5 %all-gather.9.cloned.1.call-start = ((), (), s32[]{:S(2)}) async-start(), calls=%async_computation.4 | async-start | bytes 4456448 | tf_op jit(solution)/shard_map/all_gather | solution.py:88
  77.4 0.7 copy-start.8
  78.9 176.3 %all-gather.11.cloned.1.call-start = ((), (), s32[]{:S(2)}) async-start(), calls=%async_computation.5 | async-start | bytes 4456448 | tf_op jit(solution)/shard_map/all_gather | solution.py:89
  139.5 1.0 copy-start.9
  140.5 2.0 copy-start.2
  140.5 3.7 copy-start.3
  142.5 3.9 copy-start
  142.5 3.9 copy-start.7
  279.7 0.8 copy-start.14
  282.3 15.1 %collective-permute-start = (bf16[32,768]{1,0:T(8,128)(2,1)}, bf16[32,768]{1,0:T(8,128)(2,1)}, u32[]{:S(2)}, u32[]{:S(2)}) collective-permute-start(bf16[32,768]{1,0:T(8,128)(2,1)} %get-tuple-element.20), channel_id=1, source_target_pairs={{1,0},{2,1},{3,2},{4,3},{5,4},{6,5},{7,6},{8,7},{9,8},{10,9},{11,1... | collective-permute-start | bytes 147464 | tf_op jit(solution)/shard_map/ppermute | solution.py:21
  289.5 11.4 %all-to-all-start = ((bf16[128,16,48]{0,2,1:T(8,128)(2,1)}), bf16[128,16,48]{0,2,1:T(8,128)(2,1)S(1)}, u32[]{:S(2)}, u32[]{:S(2)}) async-start(bf16[128,16,48]{0,2,1:T(8,128)(2,1)} %bitcast.25), calls=%async_computation | async-start | bytes 393216 | tf_op jit(solution)/shard_map/all_to_all | solution.py:135
  295.1 29.4 %collective-permute-start.1 = (bf16[32,768]{1,0:T(8,128)(2,1)}, bf16[32,768]{1,0:T(8,128)(2,1)}, u32[]{:S(2)}, u32[]{:S(2)}) collective-permute-start(bf16[32,768]{1,0:T(8,128)(2,1)} %get-tuple-element.21), channel_id=1, source_target_pairs={{0,1},{1,2},{2,3},{3,4},{4,5},{5,6},{6,7},{7,8},{8,9},{9,10},{10,1... | collective-permute-start | bytes 147464 | tf_op jit(solution)/shard_map/ppermute | solution.py:20
  300.9 19.9 %all-to-all-start.1 = ((bf16[128,16,192]{0,2,1:T(8,128)(2,1)}), bf16[128,16,192]{0,2,1:T(8,128)(2,1)}, u32[]{:S(2)}, u32[]{:S(2)}) async-start(bf16[128,16,192]{0,2,1:T(8,128)(2,1)} %bitcast.165), calls=%async_computation.1 | async-start | bytes 1572864 | tf_op jit(solution)/shard_map/all_to_all | solution.py:134
  308.1 153.0 %all-reduce.4.cloned.1.call-start = ((), (), s32[]{:S(2)}) async-start(), calls=%async_computation.6 | async-start | bytes 1327104 | tf_op jit(solution)/shard_map/psum | solution.py:155
  314.5 11.8 %copy-start.10 = (f32[128,768]{1,0:T(8,128)S(1)}, f32[128,768]{1,0:T(8,128)}, u32[]{:S(2)}) copy-start(f32[128,768]{1,0:T(8,128)} %fusion.46) | copy-start | bytes 1179652
  314.5 11.8 %copy-start.13 = (f32[128,768]{1,0:T(8,128)S(1)}, f32[128,768]{1,0:T(8,128)}, u32[]{:S(2)}) copy-start(f32[128,768]{1,0:T(8,128)} %fusion.49) | copy-start | bytes 1179652
  314.5 13.6 %copy-start.6 = (f32[128,768]{1,0:T(8,128)S(1)}, f32[128,768]{1,0:T(8,128)}, u32[]{:S(2)}) copy-start(f32[128,768]{1,0:T(8,128)} %copy-done.5) | copy-start | bytes 1179652
  314.6 13.6 %copy-start.12 = (bf16[1,128,768]{2,1,0:T(8,128)(2,1)S(1)}, bf16[1,128,768]{2,1,0:T(8,128)(2,1)}, u32[]{:S(2)}) copy-start(bf16[1,128,768]{2,1,0:T(8,128)(2,1)} %param.5) | copy-start | bytes 589828
  314.6 13.6 %copy-start.15 = (f32[128,768]{1,0:T(8,128)S(1)}, f32[128,768]{1,0:T(8,128)}, u32[]{:S(2)}) copy-start(f32[128,768]{1,0:T(8,128)} %copy-done.14) | copy-start | bytes 1179652
Sparse Core Ops, SparseCore 0:
  11.3 57.1 all-gather.4
  75.5 54.6 all-gather.6
  133.0 59.3 all-gather.8
  195.4 59.7 all-gather.10
  324.6 136.4 all-reduce.3
where the time goes:
time: 472 us; the launch traced here: 471 us
  waiting for transfers between devices  287 us (61%)
  matrix products  81.4 us (17%)
  blocking collectives  46.9 us (10%)
  starting transfers between devices  19.1 us (4%)
  between operations  14.1 us (3%)
  local copies, waits for them, and re-layouts  11.9 us (3%)
  other arithmetic  11.1 us (2%)
    psum x1, waiting for transfers between devices, body(): lax.psum(convolved_partial.astype(jnp.bfloat16), 'dp').astype(jnp.float32)  130 us
    all_gather x1, waiting for transfers between devices, body(): lax.all_gather(activated_low_precision, 'seq', axis=0, tiled=True)  59.5 us
    all_gather x1, waiting for transfers between devices, body(): normed_all = lax.all_gather(normed_bf, 'seq', axis=0, tiled=True)  49.5 us
    all_gather x1, waiting for transfers between devices, body(): lax.all_gather(grad_heads, 'seq', axis=0, tiled=True)  40.5 us
    all_gather x1, blocking collectives, body(): lax.all_gather(log_total[..., 0].T, 'seq', axis=0, tiled=True)  24.3 us
    all_gather x1, blocking collectives, body(): lax.all_gather(row_dots, 'seq', axis=0, tiled=True)  22.6 us
    dot_general x5, matrix products, body(): lax.dot_general(border_rows[tap_offset:tap_offset + local_rows], convolut...  11.4 us
    dot_general x1, matrix products, body(): jnp.einsum('hqk,qhd->khd', far_scores_bf, query_all, preferred_element_ty...  11.3 us
  transfers between devices with their start and end apart: 9, of which 6 were waited for; matrix products, arithmetic and copies ran while one was open for 13% of the time, Pallas kernels for 0%

commit v1 on v0

v1 whole, which is shorter than its diff:
```python
import functools

import jax
import jax.numpy as jnp
from jax import lax
from jax.experimental import pallas as pl
from jax.experimental.pallas import tpu as pltpu
from jax.sharding import PartitionSpec as P

CH = 768
HEADS = 8
HD = 128
TAPS = 5
GAP = 16
HALO = 32
ROWS = 128
SEQ = 16
DP = 16
CHIPS = 8
TILE = 256
TEMPER = HD ** (-0.5)
LOG2E = 1.4426950408889634
GELU_A = 0.7978845608028654
GELU_B = 0.044715
BF = jnp.bfloat16
F32 = jnp.float32
MESH = pl.DeviceIdType.MESH


def rcopy(src, dst, ss, rs, dev):
    return pltpu.make_async_remote_copy(
        src_ref=src, dst_ref=dst, send_sem=ss, recv_sem=rs, device_id=dev, device_id_type=MESH
    )


def dot(a, b):
    return jnp.dot(a, b, preferred_element_type=F32)


def dot_nt(a, b):
    return lax.dot_general(a, b, (((1,), (1,)), ((), ())), preferred_element_type=F32)


def flip(a):
    return a.astype(F32).T


def kernel(
    x_ref, gain_ref, og_ref, cw_hbm, w_hbm,
    att_ref, gi_ref, ct_out, gq_out,
    cwv, wfull, wh, act, normed_s, inv_s, nh, doh, qh, kv, kvt, s_ref, dkv, pr,
    odq, gsrc, gt, res, ah, gtf, gst, grcv, gown, gq, bext, bst, bh, bt, cg, cst, crcv, ct,
    rc, rq, cfin, gfin,
    wsem, hs, hr, dos, dor, nhs, nhr, kvs, kvr, ahs, ahr, os_, or_, ks, kr, prs, prr,
    gps, gpr, gus, gur, h2s, h2r, bs, br, cps, cpr, rcs, rcr, rqs, rqr, fcs, fcr, fqs, fqr,
):
    j = lax.axis_index("seq")
    d = lax.axis_index("dp")
    c = j // 2
    k = j % 2
    mate = {"seq": j + 1 - 2 * k}

    def same(chip):
        return {"seq": chip * 2 + k}

    order = (2, 0, 1, 3, 4)
    cw_copies = {t: pltpu.make_async_copy(cw_hbm.at[t], cwv.at[t], wsem.at[t]) for t in order}
    for t in order:
        cw_copies[t].start()
    col = pl.multiple_of(c * HD, HD)
    wh_copies = [
        pltpu.make_async_copy(
            w_hbm.at[:, pl.ds(p * HEADS * HD + col, HD)], wh.at[:, pl.ds(p * HD, HD)], wsem.at[5 + p]
        )
        for p in range(3)
    ]
    for cp in wh_copies:
        cp.start()
    wf_copy = pltpu.make_async_copy(w_hbm, wfull, wsem.at[8])
    wf_copy.start()

    barrier = pltpu.get_barrier_semaphore()

    def hello(i, carry):
        pl.semaphore_signal(barrier, inc=1, device_id={"seq": (j + i) % SEQ}, device_id_type=MESH)
        pl.semaphore_signal(barrier, inc=1, device_id={"dp": (d + i) % DP}, device_id_type=MESH)
        return carry

    lax.fori_loop(1, 16, hello, 0)

    x = x_ref[...].astype(F32)
    th = jnp.tanh(GELU_A * (x + GELU_B * x * x * x))
    act[HALO : HALO + ROWS, :] = (0.5 * x * (1.0 + th)).astype(BF)

    @pl.when(j == 0)
    def _():
        act[0:HALO, :] = jnp.zeros((HALO, CH), BF)
        bext[0:HALO, :] = jnp.zeros((HALO, CH), BF)

    @pl.when(j == SEQ - 1)
    def _():
        act[HALO + ROWS :, :] = jnp.zeros((HALO, CH), BF)
        bext[HALO + ROWS :, :] = jnp.zeros((HALO, CH), BF)

    pl.semaphore_wait(barrier, 30)

    def halo(buf, ss, rs):
        up = rcopy(buf.at[ROWS : ROWS + HALO], buf.at[0:HALO], ss.at[0], rs.at[0], {"seq": (j + 1) % SEQ})
        down = rcopy(
            buf.at[HALO : 2 * HALO], buf.at[HALO + ROWS : 2 * HALO + ROWS], ss.at[1], rs.at[1],
            {"seq": (j + SEQ - 1) % SEQ},
        )

        def start():
            pl.when(j < SEQ - 1)(up.start)
            pl.when(j > 0)(down.start)

        def wait_recv():
            pl.when(j > 0)(up.wait_recv)
            pl.when(j < SEQ - 1)(down.wait_recv)

        def wait_send():
            pl.when(j < SEQ - 1)(up.wait_send)
            pl.when(j > 0)(down.wait_send)

        return start, wait_recv, wait_send

    h_start, h_recv, h_send = halo(act, hs, hr)
    h_start()

    def do_copy(r):
        b = (c + r) % CHIPS
        src = og_ref.at[:, pl.ds(pl.multiple_of(b * HD, HD), HD)]
        return rcopy(src, doh.at[c], dos.at[b], dor.at[c], same(b))

    for r in range(1, CHIPS):
        do_copy(r).start()
    doh[c] = og_ref[:, pl.ds(col, HD)]

    cw_copies[2].wait()
    conv = dot(act[HALO : HALO + ROWS, :], cwv[2])
    h_recv()
    for t in (0, 1, 3, 4):
        cw_copies[t].wait()
        conv = conv + dot(act[t * GAP : t * GAP + ROWS, :], cwv[t])
    hidden = x_ref[...].astype(F32) + conv
    inv = lax.rsqrt(jnp.mean(hidden * hidden, -1, keepdims=True) + 1e-6)
    normed = hidden * inv
    normed_s[...] = normed
    inv_s[...] = jnp.broadcast_to(inv, (ROWS, HD))
    nh[c] = (normed * gain_ref[...]).astype(BF)

    def nh_copy(r):
        b = (c + r) % CHIPS
        return rcopy(nh.at[c], nh.at[c], nhs.at[b], nhr.at[c], same(b))

    def nh_wait(b):
        rcopy(nh.at[b], nh.at[b], nhs.at[b], nhr.at[b], same(b)).wait_recv()

    for r in range(1, CHIPS):
        nh_copy(r).start()

    for cp in wh_copies:
        cp.wait()

    def kv_copy(b):
        return rcopy(kv.at[k, b], kv.at[k, b], kvs.at[b], kvr.at[b], mate)

    def project(b):
        out = dot(nh[b], wh[...]).astype(BF)
        qh[b] = out[:, :HD]
        kv[k, b] = out[:, HD:]
        kv_copy(b).start()
        lane = pl.multiple_of(k * (CHIPS * ROWS) + b * ROWS, ROWS)
        kvt[0, :, pl.ds(lane, ROWS)] = flip(out[:, HD : 2 * HD]).astype(BF)
        kvt[1, :, pl.ds(lane, ROWS)] = flip(out[:, 2 * HD :]).astype(BF)

    project(c)

    def project_next(i, carry):
        b = (c + CHIPS - i) % CHIPS
        nh_wait(b)
        project(b)
        return carry

    lax.fori_loop(1, CHIPS, project_next, 0)

    mine = act.at[HALO : HALO + ROWS]

    def ah_copy(r):
        b = (c + r) % CHIPS
        return rcopy(mine, ah.at[c], ahs.at[b], ahr.at[c], same(b))

    for r in range(1, CHIPS):
        ah_copy(r).start()
    ah[c] = act[HALO : HALO + ROWS, :]

    dkv[...] = jnp.zeros_like(dkv)

    def other_keys(b, carry):
        rcopy(kv.at[1 - k, b], kv.at[1 - k, b], kvs.at[b], kvr.at[b], mate).wait_recv()
        lane = pl.multiple_of((1 - k) * (CHIPS * ROWS) + b * ROWS, ROWS)
        kvt[0, :, pl.ds(lane, ROWS)] = flip(kv[1 - k, b, :, :HD]).astype(BF)
        kvt[1, :, pl.ds(lane, ROWS)] = flip(kv[1 - k, b, :, HD:]).astype(BF)
        return carry

    lax.fori_loop(0, CHIPS, other_keys, 0)
    for r in range(1, CHIPS):
        b = (c + r) % CHIPS
        rcopy(doh.at[b], doh.at[b], dos.at[b], dor.at[b], same(b)).wait_recv()

    def chunk(i, half):
        two = kv[i // 4, (i % 4) * 2 : (i % 4) * 2 + 2, :, half * HD : (half + 1) * HD]
        return two.reshape(TILE, HD)

    def odq_copy(b):
        return rcopy(
            odq.at[:, b], res.at[0:2, :, pl.ds(col, HD)], os_.at[b], or_.at[c], same(b)
        )

    def tile(t, carry):
        b0 = (c + 1 + 2 * t) % CHIPS
        b1 = (c + 2 + 2 * t) % CHIPS
        q = jnp.concatenate([qh[b0], qh[b1]], axis=0)
        go = jnp.concatenate([doh[b0], doh[b1]], axis=0)
        qt = flip(q).astype(BF)
        got_f = flip(go)
        got = got_f.astype(BF)
        top = None
        for i in range(8):
            s = dot(chunk(i, 0), qt)
            s_ref[i * TILE : (i + 1) * TILE, :] = s
            part = jnp.max(s.reshape(TILE // 8, 8, TILE), axis=0)
            top = part if top is None else jnp.maximum(top, part)
        top = jnp.max(top, axis=0, keepdims=True) * (TEMPER * LOG2E)
        total = jnp.zeros((8, TILE), F32)
        for i in range(8):
            p = jnp.exp2(s_ref[i * TILE : (i + 1) * TILE, :] * (TEMPER * LOG2E) - top)
            s_ref[i * TILE : (i + 1) * TILE, :] = p
            total = total + jnp.sum(p.reshape(TILE // 8, 8, TILE), axis=0)
        rec = 1.0 / jnp.sum(total, axis=0, keepdims=True)
        ot = jnp.zeros((HD, TILE), F32)
        for i in range(8):
            w = s_ref[i * TILE : (i + 1) * TILE, :] * rec
            s_ref[i * TILE : (i + 1) * TILE, :] = w
            wb = w.astype(BF)
            ot = ot + dot(kvt[1, :, i * TILE : (i + 1) * TILE], wb)
            rows = pl.ds((i % 4) * TILE, TILE)
            dkv[i // 4, rows, HD:] = dkv[i // 4, rows, HD:] + dot(wb, go)
        otb = ot.astype(BF).astype(F32)
        dots = jnp.sum(got_f * otb, axis=0, keepdims=True)
        dqt = jnp.zeros((HD, TILE), F32)
        for i in range(8):
            gw = dot(chunk(i, 1), got)
            ds = (s_ref[i * TILE : (i + 1) * TILE, :] * (gw - dots)).astype(BF)
            dqt = dqt + dot(kvt[0, :, i * TILE : (i + 1) * TILE], ds)
            rows = pl.ds((i % 4) * TILE, TILE)
            dkv[i // 4, rows, :HD] = dkv[i // 4, rows, :HD] + dot(ds, q)
        dqt = dqt * TEMPER
        o = otb.T.astype(BF)
        dq = dqt.T.astype(BF)
        dqtb = dqt.astype(BF)
        odq[0, b0] = o[:ROWS]
        odq[0, b1] = o[ROWS:]
        odq[1, b0] = dq[:ROWS]
        odq[1, b1] = dq[ROWS:]
        gt[0:HD, pl.ds(pl.multiple_of(b0 * ROWS, ROWS), ROWS)] = dqtb[:, :ROWS]
        gt[0:HD, pl.ds(pl.multiple_of(b1 * ROWS, ROWS), ROWS)] = dqtb[:, ROWS:]
        odq_copy(b0).start()

        @pl.when(t < 3)
        def _():
            odq_copy(b1).start()

        return carry

    lax.fori_loop(0, 4, tile, 0)
    res[0, :, pl.ds(col, HD)] = odq[0, c]
    res[1, :, pl.ds(col, HD)] = odq[1, c]

    pr_copy = rcopy(dkv.at[1 - k], pr, prs.at[0], prr.at[0], mate)
    pr_copy.start()
    pr_copy.wait_recv()

    def dkv_copy(b):
        return rcopy(
            gsrc.at[:, b], res.at[2:4, :, pl.ds(col, HD)], ks.at[b], kr.at[c], same(b)
        )

    def give_back(i, carry):
        b = (c + 1 + i) % CHIPS
        rows = pl.ds(pl.multiple_of(b * ROWS, ROWS), ROWS)
        both = dkv[k, rows, :] + pr[rows, :]
        dk = both[:, :HD] * TEMPER
        dv = both[:, HD:]
        gsrc[0, b] = dk.astype(BF)
        gsrc[1, b] = dv.astype(BF)

        @pl.when(i < CHIPS - 1)
        def _():
            dkv_copy(b).start()

        gt[HD : 2 * HD, rows] = dk.T.astype(BF)
        gt[2 * HD :, rows] = dv.T.astype(BF)
        return carry

    lax.fori_loop(0, CHIPS, give_back, 0)
    res[2, :, pl.ds(col, HD)] = gsrc[0, c]
    res[3, :, pl.ds(col, HD)] = gsrc[1, c]

    gtf[...] = dot(gt[...], nh[...].reshape(CHIPS * ROWS, CH))
    for p in range(3):
        rows = pl.ds(pl.multiple_of(p * HD + (1 - k) * 64, 64), 64)
        gst[p] = gtf[rows, :].astype(BF).reshape(4, 16, CH)
    gp_copy = rcopy(gst, grcv, gps.at[0], gpr.at[0], mate)
    gp_copy.start()

    for r in range(1, CHIPS):
        b = (c + r) % CHIPS
        lanes = pl.ds(pl.multiple_of(b * HD, HD), HD)
        rcopy(odq.at[:, b], res.at[0:2, :, lanes], os_.at[b], or_.at[b], same(b)).wait_recv()
        rcopy(gsrc.at[:, b], res.at[2:4, :, lanes], ks.at[b], kr.at[b], same(b)).wait_recv()
    att_ref[...] = res[0]
    wf_copy.wait()
    inner = HEADS * HD
    gn = dot_nt(res[1], wfull[:, :inner])
    gn = gn + dot_nt(res[2], wfull[:, inner : 2 * inner])
    gn = gn + dot_nt(res[3], wfull[:, 2 * inner :])
    scaled = gn * gain_ref[...]
    nrm = normed_s[...]
    gh = inv_s[:, 0:1] * (scaled - nrm * jnp.mean(scaled * nrm, -1, keepdims=True))
    normed_s[...] = gh
    bext[HALO : HALO + ROWS, :] = gh.astype(BF)
    b_start, b_recv, b_send = halo(bext, h2s, h2r)
    b_start()

    gp_copy.wait_recv()
    for p in range(3):
        rows = pl.ds(pl.multiple_of(p * HD + k * 64, 64), 64)
        gown[p] = (gtf[rows, :].reshape(4, 16, CH) + grcv[p].astype(F32)).astype(BF)
        unit = SEQ * p + j
        owner = unit // 3
        slot = unit % 3

        @pl.when(owner == j)
        def _():
            gq[pl.ds(slot * 4, 4)] = gown[p]

        @pl.when(owner != j)
        def _():
            rcopy(gown.at[p], gq.at[pl.ds(slot * 4, 4)], gus.at[p], gur.at[slot], {"seq": owner}).start()

    b_recv()
    wide = bext[...].astype(F32)
    for b in range(CHIPS):
        turned = wide if b == 0 else pltpu.roll(wide, CH - 96 * b, 1)
        bst[b] = turned[:, :HD].astype(BF)

    def b_copy(r):
        b = (c + r) % CHIPS
        return rcopy(bst.at[b], bh.at[c], bs.at[b], br.at[c], same(b))

    for r in range(1, CHIPS):
        b_copy(r).start()
    bh[c] = bst[c]

    ga = dot_nt(bext[(TAPS - 1) * GAP : (TAPS - 1) * GAP + ROWS, :], cwv[0])
    for t in range(1, TAPS):
        lo = (TAPS - 1 - t) * GAP
        ga = ga + dot_nt(bext[lo : lo + ROWS, :], cwv[t])
    x = x_ref[...].astype(F32)
    th = jnp.tanh(GELU_A * (x + GELU_B * x * x * x))
    slope = 0.5 * (1.0 + th) + 0.5 * x * (1.0 - th * th) * GELU_A * (1.0 + 3.0 * GELU_B * x * x)
    gi_ref[...] = (normed_s[...] + slope * ga).astype(BF)

    for slot in range(3):
        @pl.when((3 * j + slot) % SEQ != j)
        def _():
            rcopy(gown.at[0], gq.at[pl.ds(slot * 4, 4)], gus.at[0], gur.at[slot], mate).wait_recv()

    def rq_copy(i):
        to = (d + i) % DP
        return rcopy(gq.at[jnp.minimum(15 - to, 11)], rq.at[d], rqs.at[to], rqr.at[d], {"dp": to}), to

    def rq_send(i, carry):
        cp, to = rq_copy(i)
        pl.when(to >= 4)(cp.start)
        return carry

    lax.fori_loop(1, DP, rq_send, 0)

    for r in range(1, CHIPS):
        b = (c + r) % CHIPS
        rcopy(ah.at[b], ah.at[b], ahs.at[b], ahr.at[b], same(b)).wait_recv()
        rcopy(bh.at[b], bh.at[b], bs.at[b], br.at[b], same(b)).wait_recv()
    for t in range(TAPS):
        lo = (TAPS - 1 - t) * GAP
        win = bh[:, lo : lo + ROWS, :].reshape(CHIPS * ROWS, HD)
        bt[t * 96 : (t + 1) * 96, :] = flip(win)[:96].astype(BF)
    cg[...] = dot(bt[...], ah[...].reshape(CHIPS * ROWS, CH))
    for t in range(TAPS):
        rows = pl.ds(pl.multiple_of(t * 96 + (1 - k) * 48, 48), 48)
        cst[t * 3 : t * 3 + 3] = cg[rows, :].astype(BF).reshape(3, 16, CH)
    cp_copy = rcopy(cst, crcv, cps.at[0], cpr.at[0], mate)
    cp_copy.start()

    def take(buf, ss, rs):
        def step(i, carry):
            frm = (d + i) % DP
            rcopy(buf.at[frm], buf.at[frm], ss.at[frm], rs.at[frm], {"dp": frm}).wait_recv()
            return carry

        lax.fori_loop(1, DP, step, 0)
        total = buf[0].astype(F32)
        for i in range(1, DP):
            total = total + buf[i].astype(F32)
        return total.astype(BF)

    def spread(buf, mine, ss, rs):
        def step(i, carry):
            to = (d + i) % DP
            rcopy(buf.at[mine], buf.at[mine], ss.at[to], rs.at[mine], {"dp": to}).start()
            return carry

        lax.fori_loop(1, DP, step, 0)

    @pl.when(d >= 4)
    def _():
        rq[d] = gq[15 - d]
        gfin[15 - d] = take(rq, rqs, rqr)
        spread(gfin, 15 - d, fqs, fqr)

    cp_copy.wait_recv()
    for t in range(TAPS):
        rows = pl.ds(pl.multiple_of(t * 96 + k * 48, 48), 48)
        own = cg[rows, :].reshape(3, 16, CH)
        ct[t * 3 : t * 3 + 3] = (own + crcv[t * 3 : t * 3 + 3].astype(F32)).astype(BF)

    def rc_copy(i):
        to = (d + i) % DP
        return rcopy(ct.at[jnp.minimum(to, 14)], rc.at[d], rcs.at[to], rcr.at[d], {"dp": to}), to

    def rc_send(i, carry):
        cp, to = rc_copy(i)
        pl.when(to < 15)(cp.start)
        return carry

    lax.fori_loop(1, DP, rc_send, 0)

    @pl.when(d < 15)
    def _():
        rc[d] = ct[d]
        cfin[d] = take(rc, rcs, rcr)
        spread(cfin, d, fcs, fcr)

    def land(i, carry):
        frm = (d + i) % DP

        @pl.when(frm >= 4)
        def _():
            m = 15 - frm
            rcopy(gfin.at[m], gfin.at[m], fqs.at[frm], fqr.at[m], {"dp": frm}).wait_recv()

        return carry

    lax.fori_loop(1, DP, land, 0)
    gq_out[...] = gfin[...].astype(F32).reshape(192, CH)

    def land_c(i, carry):
        frm = (d + i) % DP

        @pl.when(frm < 15)
        def _():
            rcopy(cfin.at[frm], cfin.at[frm], fcs.at[frm], fcr.at[frm], {"dp": frm}).wait_recv()

        return carry

    lax.fori_loop(1, DP, land_c, 0)
    ct_out[...] = cfin[...].astype(F32).reshape(240, CH)

    h_send()
    b_send()
    pr_copy.wait_send()
    gp_copy.wait_send()
    cp_copy.wait_send()
    for r in range(1, CHIPS):
        do_copy(r).wait_send()
        nh_copy(r).wait_send()
        ah_copy(r).wait_send()
        b_copy(r).wait_send()
        b = (c + r) % CHIPS
        odq_copy(b).wait_send()
        dkv_copy(b).wait_send()
    for b in range(CHIPS):
        kv_copy(b).wait_send()
    for p in range(3):
        unit = SEQ * p + j

        @pl.when(unit // 3 != j)
        def _():
            rcopy(gown.at[p], gq.at[pl.ds(0, 4)], gus.at[p], gur.at[0], {"seq": unit // 3}).wait_send()

    def drain(i, carry):
        cp, to = rq_copy(i)
        pl.when(to >= 4)(cp.wait_send)
        cp, to = rc_copy(i)
        pl.when(to < 15)(cp.wait_send)

        @pl.when(d >= 4)
        def _():
            rcopy(gfin.at[0], gfin.at[0], fqs.at[to], fqr.at[0], {"dp": to}).wait_send()

        @pl.when(d < 15)
        def _():
            rcopy(cfin.at[0], cfin.at[0], fcs.at[to], fcr.at[0], {"dp": to}).wait_send()

        return carry

    lax.fori_loop(1, DP, drain, 0)


def body(inputs, convolution_weight, w_qkv, gain, out_grad):
    vm = pl.BlockSpec(memory_space=pltpu.VMEM)
    hbm = pl.BlockSpec(memory_space=pl.ANY)
    V = pltpu.VMEM

    def sem(n):
        return pltpu.SemaphoreType.DMA((n,))

    half = CHIPS * ROWS
    scratch = [
        V((TAPS, CH, CH), BF),
        V((CH, 3 * HEADS * HD), BF),
        V((CH, 3 * HD), BF),
        V((ROWS + 2 * HALO, CH), BF),
        V((ROWS, CH), F32),
        V((ROWS, HD), F32),
        V((CHIPS, ROWS, CH), BF),
        V((CHIPS, ROWS, HD), BF),
        V((CHIPS, ROWS, HD), BF),
        V((2, CHIPS, ROWS, 2 * HD), BF),
        V((2, HD, 2 * half), BF),
        V((2 * half, TILE), F32),
        V((2, half, 2 * HD), F32),
        V((half, 2 * HD), F32),
        V((2, CHIPS, ROWS, HD), BF),
        V((2, CHIPS, ROWS, HD), BF),
        V((3 * HD, half), BF),
        V((4, ROWS, HEADS * HD), BF),
        V((CHIPS, ROWS, CH), BF),
        V((3 * HD, CH), F32),
        V((3, 4, 16, CH), BF),
        V((3, 4, 16, CH), BF),
        V((3, 4, 16, CH), BF),
        V((12, 16, CH), BF),
        V((ROWS + 2 * HALO, CH), BF),
        V((CHIPS, ROWS + 2 * HALO, HD), BF),
        V((CHIPS, ROWS + 2 * HALO, HD), BF),
        V((TAPS * 96, half), BF),
        V((TAPS * 96, CH), F32),
        V((15, 16, CH), BF),
        V((15, 16, CH), BF),
        V((15, 16, CH), BF),
        V((DP, 16, CH), BF),
        V((DP, 16, CH), BF),
        V((15, 16, CH), BF),
        V((12, 16, CH), BF),
        sem(9),
        sem(2), sem(2), sem(8), sem(8), sem(8), sem(8), sem(8), sem(8), sem(8), sem(8),
        sem(8), sem(8), sem(8), sem(8), sem(1), sem(1),
        sem(1), sem(1), sem(3), sem(3), sem(2), sem(2), sem(8), sem(8), sem(1), sem(1),
        sem(16), sem(16), sem(16), sem(16), sem(16), sem(16), sem(16), sem(16),
    ]
    att, gi, ct, gq = pl.pallas_call(
        kernel,
        out_shape=[
            jax.ShapeDtypeStruct((ROWS, HEADS * HD), BF),
            jax.ShapeDtypeStruct((ROWS, CH), BF),
            jax.ShapeDtypeStruct((240, CH), F32),
            jax.ShapeDtypeStruct((192, CH), F32),
        ],
        in_specs=[vm, vm, vm, hbm, hbm],
        out_specs=[vm, vm, vm, vm],
        scratch_shapes=scratch,
        compiler_params=pltpu.CompilerParams(
            collective_id=0, has_side_effects=True, vmem_limit_bytes=56 * 1024 * 1024
        ),
        cost_estimate=pl.CostEstimate(flops=8_000_000_000, bytes_accessed=15_000_000, transcendentals=2_200_000),
    )(inputs[0], gain[None, :], out_grad[0], convolution_weight, w_qkv)
    conv = ct.reshape(TAPS, 48, CH).transpose(0, 2, 1)
    return att[None], gi[None], conv, gq.T


def solution(mesh):
    in_specs = (P("dp", "seq", None), P(), P(), P(), P("dp", "seq", None))
    out_specs = (P("dp", "seq", None), P("dp", "seq", None), P(None, None, "seq"), P(None, "seq"))
    return jax.shard_map(body, mesh=mesh, in_specs=in_specs, out_specs=out_specs, check_vma=False)
```

time: 472 us -> 133 us (0.28)
  the two profiles are of different devices: /device:TPU:6 before, /device:TPU:1 now
where the time goes in v1:
time: 133 us; the launch traced here: 131 us
  Pallas kernels  122 us (92%)
  local copies, waits for them, and re-layouts  8.49 us (6%)
    pallas_call x1, Pallas kernels, body(): pl.pallas_call(kernel, out_shape=[jax.ShapeDtypeStruct((ROWS, HEADS * HD)...  122 us
    unnamed x4, local copies, waits for them, and re-layouts  7.23 us

profile of v1, /device:TPU:1, one launch (start us, length us, event | category | flops | bytes accessed | tf_op | source)
XLA Modules:
  0.0 130.9 jit_solution(3056200642104384434)
XLA Ops:
  0.6 1.3 broadcast_in_dim.9.gain_ref
  1.9 121.8 %shard_map.84 = (bf16[128,1024]{1,0:T(8,128)(2,1)}, bf16[128,768]{1,0:T(8,128)(2,1)}, f32[240,768]{1,0:T(8,128)}, f32[192,768]{1,0:T(8,128)}) custom-call(bf16[128,768]{1,0:T(8,128)(2,1)} %bitcast.13, f32[1,768]{1,0:T(1,128)} %broadcast_in_dim.9.gain_ref, bf16[128,1024]{1,0:T(8,128)(2,1)} %bitcast.12, bf16[5,768,768]{2,1,0:T(8,128)(2,1)} %cw_hbm.1, ...), custom_call_target="tpu_custom_call" | custom-call | flops 8000000000 | bytes 15000000 | tf_op jit(solution)/shard_map/pallas_call | solution.py:574
  123.7 1.7 %copy.13 = bf16[1,128,1024]{2,1,0:T(8,128)(2,1)} copy(bf16[1,128,1024]{2,1,0:T(8,128)(2,1)} %bitcast.10) | data formatting | bytes 524288
  125.3 1.6 %copy.14 = bf16[1,128,768]{2,1,0:T(8,128)(2,1)} copy(bf16[1,128,768]{2,1,0:T(8,128)(2,1)} %bitcast.11) | data formatting | bytes 393216
  127.0 2.0 %copy.15 = f32[5,768,48]{1,2,0:T(8,128)} copy(f32[5,768,48]{1,2,0:T(8,128)} %bitcast.8) | data formatting | bytes 1474560
  129.0 1.9 %copy.16 = f32[768,192]{0,1:T(8,128)} copy(f32[768,192]{0,1:T(8,128)} %bitcast.9) | data formatting | bytes 1179648

commit v2 on v0

v2 whole, which is shorter than its diff:
```python
import jax
import jax.numpy as jnp
from jax import lax
from jax.experimental import pallas as pl
from jax.experimental.pallas import tpu as pltpu
from jax.sharding import PartitionSpec as P

CH = 768
HEADS = 8
HD = 128
INNER = HEADS * HD
TAPS = 5
GAP = 16
HALO = 32
ROWS = 128
SEQ = 16
DP = 16
CHIPS = 8
HALF = CHIPS * ROWS
TILE = 256
TILES = HALF // TILE
PART = 384
GROUPS = 3
WIDE = CH // GROUPS
TEMPER = HD ** (-0.5)
LOG2E = 1.4426950408889634
GELU_A = 0.7978845608028654
GELU_B = 0.044715
BF = jnp.bfloat16
F32 = jnp.float32
MESH = pl.DeviceIdType.MESH


def rcopy(src, dst, ss, rs, dev):
    return pltpu.make_async_remote_copy(
        src_ref=src, dst_ref=dst, send_sem=ss, recv_sem=rs, device_id=dev, device_id_type=MESH
    )


def dot(a, b):
    return jnp.dot(a, b, preferred_element_type=F32)


def dot_nt(a, b):
    return lax.dot_general(a, b, (((1,), (1,)), ((), ())), preferred_element_type=F32)


def flip(a):
    return a.astype(F32).T


def gelu_tanh(x):
    return jnp.tanh(GELU_A * (x + GELU_B * x * x * x))


def gelu(x):
    x = x.astype(F32)
    return (0.5 * x * (1.0 + gelu_tanh(x))).astype(BF)


def loop(n, step):
    lax.fori_loop(0, n, lambda i, carry: (step(i), carry)[1], 0)


def kernel(
    x_ref, gain_ref, og_ref, cw_hbm, w_hbm,
    att_ref, gi_ref, cfin, gfin,
    cwv, wfull, wh, xg, xhb, ag, acc_s, hbuf, hid_s, nh, doh, dot_s, qd, qt_s, kv, kt_s, vt_s,
    wts, stat_s, dor_s, dqt, dkvp, pr, obuf, dqb, gsrc, gt, res, gtf, gst, grcv, gown,
    rq, red, bext, bst, bh, bt, cg, cst, crcv, ct, rc,
    wsem, xs, xr, xhs, xhr, dos, dor, hds, hdr, kvs, kvr, os_, or_, dqs, dqr, ks, kr, prs, prr,
    gps, gpr, rqs, rqr, gus, gur, h2s, h2r, bs, br, cps, cpr, rcs, rcr, fcs, fcr,
):
    j = lax.axis_index("seq")
    d = lax.axis_index("dp")
    c = j // 2
    k = j % 2
    mate = {"seq": j + 1 - 2 * k}
    home = j // CHIPS
    slot = j % CHIPS
    col = pl.multiple_of(c * HD, HD)

    for t in range(TAPS):
        pltpu.make_async_copy(cw_hbm.at[t], cwv.at[t], wsem.at[t]).start()
    for p in range(3):
        pltpu.make_async_copy(
            w_hbm.at[:, pl.ds(p * INNER + col, HD)], wh.at[:, pl.ds(p * HD, HD)], wsem.at[5 + p]
        ).start()
    wf_copy = pltpu.make_async_copy(w_hbm, wfull, wsem.at[8])
    wf_copy.start()

    barrier = pltpu.get_barrier_semaphore()

    def hello(i):
        pl.semaphore_signal(barrier, inc=1, device_id={"seq": (j + i + 1) % SEQ}, device_id_type=MESH)
        pl.semaphore_signal(barrier, inc=1, device_id={"dp": (d + i + 1) % DP}, device_id_type=MESH)

    loop(15, hello)
    dqt[...] = jnp.zeros_like(dqt)
    pl.semaphore_wait(barrier, 30)

    def to_worker(copy, local):
        def step(i):
            chip = (c + CHIPS - 1 - i) % CHIPS
            dev = 2 * chip + home

            @pl.when(dev != j)
            def _():
                copy(chip, {"seq": dev}).start()

            if local is not None:
                pl.when(dev == j)(lambda: local(chip))

        loop(CHIPS, step)

    def to_worker_done(copy):
        def step(chip):
            dev = 2 * chip + home

            @pl.when(dev != j)
            def _():
                copy(chip, {"seq": dev}).wait_send()

        loop(CHIPS, step)

    def owner_of(b):
        return CHIPS * k + b

    def xh_copy(chip):
        start = pl.multiple_of(96 * (8 - j), HALO)
        return rcopy(
            x_ref.at[pl.ds(start, HALO)], xhb, xhs.at[chip], xhr.at[0], {"seq": 2 * chip + 8 - j}
        )

    @pl.when((j == 7) | (j == 8))
    def _():
        def step(i):
            chip = (c + CHIPS - 1 - i) % CHIPS

            @pl.when(chip != c)
            def _():
                xh_copy(chip).start()

        loop(CHIPS, step)

    pl.when(j == 7)(lambda: xhb.__setitem__(Ellipsis, x_ref[ROWS - HALO :, :]))
    pl.when(j == 8)(lambda: xhb.__setitem__(Ellipsis, x_ref[:HALO, :]))

    def x_copy(g):
        def copy(chip, dev):
            src = x_ref.at[:, g * WIDE : (g + 1) * WIDE]
            return rcopy(src, xg.at[g, slot], xs.at[g, chip], xr.at[g, slot], dev)

        return copy

    for g in range(GROUPS):
        def x_local(chip, g=g):
            xg[g, slot] = x_ref[:, g * WIDE : (g + 1) * WIDE]

        to_worker(x_copy(g), x_local)

    def do_copy(chip, dev):
        src = og_ref.at[:, pl.ds(pl.multiple_of(chip * HD, HD), HD)]
        return rcopy(src, doh.at[slot], dos.at[chip], dor.at[slot], dev)

    def do_local(chip):
        doh[slot] = og_ref[:, pl.ds(pl.multiple_of(chip * HD, HD), HD)]

    to_worker(do_copy, do_local)

    def wait_slot(buf, ss, rs, b):
        @pl.when(owner_of(b) != j)
        def _():
            rcopy(buf.at[b], buf.at[b], ss.at[0], rs.at[b], mate).wait_recv()

    def kv_copy(p):
        return rcopy(kv.at[k, p], kv.at[k, p], kvs.at[p], kvr.at[p], mate)

    def finish_rows(p, acc):
        inv = lax.rsqrt(jnp.mean(acc * acc, -1, keepdims=True) + 1e-6)

        @pl.when((k == c // 4) & (p == c % 4))
        def _():
            hbuf[...] = acc.reshape(2, ROWS, CH)

        rows_bf = (acc * inv * gain_ref[...]).astype(BF)
        nh[p] = rows_bf
        outb = dot(rows_bf, wh[...]).astype(BF)
        kv[k, p] = outb[:, HD:]
        kv_copy(p).start()
        qd[pl.ds(pl.multiple_of(p * TILE, TILE), TILE), :] = outb[:, :HD]
        outf = outb.astype(F32)
        qt_s[p] = outf[:, :HD].T.astype(BF)
        kt_s[k * TILES + p] = outf[:, HD : 2 * HD].T.astype(BF)
        vt_s[k * TILES + p] = outf[:, 2 * HD :].T.astype(BF)

    @pl.when((j != 7) & (j != 8))
    def _():
        rcopy(xhb, xhb, xhs.at[0], xhr.at[0], mate).wait_recv()

    edge = gelu(xhb[...])
    ag[0:HALO, :] = jnp.where(k == 1, edge, jnp.zeros_like(edge))
    ag[HALO + HALF :, :] = jnp.where(k == 0, edge, jnp.zeros_like(edge))
    for t in range(TAPS):
        pltpu.make_async_copy(cw_hbm.at[t], cwv.at[t], wsem.at[t]).wait()
    for p in range(3):
        pltpu.make_async_copy(
            w_hbm.at[:, pl.ds(p * INNER + col, HD)], wh.at[:, pl.ds(p * HD, HD)], wsem.at[5 + p]
        ).wait()
    for g in range(GROUPS):
        lanes = slice(g * WIDE, (g + 1) * WIDE)

        def arrive(p, g=g, lanes=lanes):
            for e in range(2):
                wait_slot(xg.at[g], xs.at[g], xr.at[g], 2 * p + e)
            block = xg[g, pl.ds(2 * p, 2)].reshape(TILE, WIDE)
            ag[pl.ds(pl.multiple_of(HALO + p * TILE, HALO), TILE), lanes] = gelu(block)
            if g == 0:
                acc_s[p] = jnp.zeros((TILE, CH), F32)
            acc_s[p, :, lanes] = acc_s[p, :, lanes] + block.astype(F32)

        loop(TILES, arrive)

        def convolve(p, g=g, lanes=lanes):
            part = None
            for t in range(TAPS):
                rows = pl.ds(pl.multiple_of(p * TILE + t * GAP, GAP), TILE)
                one = dot(ag[rows, lanes], cwv[t, lanes, :])
                part = one if part is None else part + one
            if g < GROUPS - 1:
                acc_s[p] = acc_s[p] + part
            else:
                finish_rows(p, acc_s[p] + part)

        loop(TILES, convolve)

    hd_copy = rcopy(hbuf.at[1 - k], hid_s, hds.at[0], hdr.at[0], mate)

    @pl.when(k == c // 4)
    def _():
        hd_copy.start()
        hid_s[...] = hbuf[k]

    def cotangents(t):
        for e in range(2):
            wait_slot(doh, dos, dor, 2 * t + e)
        dot_s[t] = flip(doh[pl.ds(2 * t, 2)].reshape(TILE, HD)).astype(BF)

    loop(TILES, cotangents)

    def other_keys(p):
        rcopy(kv.at[1 - k, p], kv.at[1 - k, p], kvs.at[p], kvr.at[p], mate).wait_recv()
        both = kv[1 - k, p].astype(F32)
        kt_s[(1 - k) * TILES + p] = both[:, :HD].T.astype(BF)
        vt_s[(1 - k) * TILES + p] = both[:, HD:].T.astype(BF)

    loop(TILES, other_keys)

    def give(copy, local, p):
        for e in range(2):
            b = 2 * p + e
            pl.when(owner_of(b) != j)(lambda b=b: copy(b).start())
            pl.when(owner_of(b) == j)(lambda b=b: local(b))

    def o_copy(b):
        return rcopy(
            obuf.at[b], att_ref.at[:, pl.ds(col, HD)], os_.at[b], or_.at[c], {"seq": owner_of(b)}
        )

    def o_local(b):
        att_ref[:, pl.ds(col, HD)] = obuf[b]

    def forward(t):
        qt = qt_s[t]
        top = None
        for i in range(2 * TILES):
            s = dot(kv[i // TILES, i % TILES, :, :HD], qt)
            part = jnp.max(s.reshape(TILE // 8, 8, TILE), axis=0)
            top = part if top is None else jnp.maximum(top, part)
        top = jnp.max(top, axis=0, keepdims=True) * (TEMPER * LOG2E)
        total = jnp.zeros((8, TILE), F32)
        ot = jnp.zeros((HD, TILE), F32)
        lanes = pl.ds(pl.multiple_of(t * TILE, TILE), TILE)
        for i in range(2 * TILES):
            s = dot(kv[i // TILES, i % TILES, :, :HD], qt)
            p = jnp.exp2(s * (TEMPER * LOG2E) - top)
            total = total + jnp.sum(p.reshape(TILE // 8, 8, TILE), axis=0)
            pb = p.astype(BF)
            wts[i, :, lanes] = pb
            ot = ot + dot(vt_s[i], pb)
        rec = 1.0 / jnp.sum(total, axis=0, keepdims=True)
        otb = (ot * rec).astype(BF).astype(F32)
        go = dot_s[t].astype(F32)
        dots = jnp.sum(go * otb, axis=0, keepdims=True)
        stat_s[0, :, lanes] = jnp.broadcast_to(rec, (8, TILE))
        stat_s[1, :, lanes] = jnp.broadcast_to(dots, (8, TILE))
        dor_s[lanes, :] = (go * rec).T.astype(BF)
        obuf[pl.ds(2 * t, 2)] = otb.T.astype(BF).reshape(2, ROWS, HD)
        give(o_copy, o_local, t)

    loop(TILES, forward)

    def backward(h, m):
        g = h * TILES + m
        vc = kv[h, m, :, HD:]
        w = wts[g]
        parts = []
        for t in range(TILES):
            lanes = slice(t * TILE, (t + 1) * TILE)
            gw = dot(vc, dot_s[t])
            slope = (gw - stat_s[1, 0:1, lanes]) * stat_s[0, 0:1, lanes]
            parts.append((w[:, lanes].astype(F32) * slope).astype(BF))
        ds = jnp.concatenate(parts, axis=1)
        dv = dot(w, dor_s[...])
        dk = dot(ds, qd[...])
        dqt[...] = dqt[...] + dot(kt_s[g], ds)
        return dk * TEMPER, dv

    def pr_copy(m):
        return rcopy(dkvp.at[m], pr.at[m], prs.at[m], prr.at[m], mate)

    def other_half(m):
        dk, dv = backward(1 - k, m)
        dkvp[m, 0] = dk
        dkvp[m, 1] = dv
        pr_copy(m).start()

    loop(TILES, other_half)

    def kv_back(b):
        return rcopy(
            gsrc.at[:, b], res.at[1:3, :, pl.ds(col, HD)], ks.at[b], kr.at[c], {"seq": owner_of(b)}
        )

    def kv_local(b):
        res[1, :, pl.ds(col, HD)] = gsrc[0, b]
        res[2, :, pl.ds(col, HD)] = gsrc[1, b]

    def own_half(m):
        dk, dv = backward(k, m)
        pr_copy(m).wait_recv()
        dk = dk + pr[m, 0]
        dv = dv + pr[m, 1]
        gsrc[0, pl.ds(2 * m, 2)] = dk.astype(BF).reshape(2, ROWS, HD)
        gsrc[1, pl.ds(2 * m, 2)] = dv.astype(BF).reshape(2, ROWS, HD)
        give(kv_back, kv_local, m)
        gt[m, HD : 2 * HD, :] = dk.T.astype(BF)
        gt[m, 2 * HD :, :] = dv.T.astype(BF)

    loop(TILES, own_half)

    def dq_copy(b):
        return rcopy(
            dqb.at[b], res.at[0, :, pl.ds(col, HD)], dqs.at[b], dqr.at[c], {"seq": owner_of(b)}
        )

    def dq_local(b):
        res[0, :, pl.ds(col, HD)] = dqb[b]

    def query_back(t):
        dq = dqt[:, pl.ds(pl.multiple_of(t * TILE, TILE), TILE)] * TEMPER
        dqb[pl.ds(2 * t, 2)] = dq.T.astype(BF).reshape(2, ROWS, HD)
        give(dq_copy, dq_local, t)
        gt[t, :HD, :] = dq.astype(BF)

    loop(TILES, query_back)

    for t in range(TILES):
        part = dot(gt[t], nh[t])
        gtf[...] = part if t == 0 else gtf[...] + part
    for p in range(3):
        rows = pl.ds(pl.multiple_of(p * HD + (1 - k) * 64, 64), 64)
        gst[p * 4 : p * 4 + 4] = gtf[rows, :].astype(BF).reshape(4, 16, CH)
    gp_copy = rcopy(gst, grcv, gps.at[0], gpr.at[0], mate)
    gp_copy.start()
    gp_copy.wait_recv()
    for p in range(3):
        rows = pl.ds(pl.multiple_of(p * HD + k * 64, 64), 64)
        own = gtf[rows, :].reshape(4, 16, CH)
        gown[p * 4 : p * 4 + 4] = (own + grcv[p * 4 : p * 4 + 4].astype(F32)).astype(BF)

    def rq_copy(to):
        return rcopy(gown.at[jnp.minimum(15 - to, 11)], rq.at[d], rqs.at[to], rqr.at[d], {"dp": to})

    def rq_send(i):
        to = (d + 1 + i) % DP
        pl.when(to >= 4)(lambda: rq_copy(to).start())

    loop(15, rq_send)

    @pl.when(k != c // 4)
    def _():
        hd_copy.wait_recv()

    def back(copy):
        def step(i):
            chip = (c + i) % CHIPS
            lanes = pl.ds(pl.multiple_of(chip * HD, HD), HD)
            pl.when(2 * chip + home != j)(lambda: copy(chip, lanes).wait_recv())

        loop(CHIPS, step)

    wf_copy.wait()
    back(lambda chip, lanes: rcopy(gsrc.at[:, 0], res.at[1:3, :, lanes], ks.at[0], kr.at[chip], mate))
    gn = dot_nt(res[1], wfull[:, INNER : 2 * INNER])
    gn = gn + dot_nt(res[2], wfull[:, 2 * INNER :])
    back(lambda chip, lanes: rcopy(dqb.at[0], res.at[0, :, lanes], dqs.at[0], dqr.at[chip], mate))
    gn = gn + dot_nt(res[0], wfull[:, :INNER])
    hidden = hid_s[...]
    inv = lax.rsqrt(jnp.mean(hidden * hidden, -1, keepdims=True) + 1e-6)
    normed = hidden * inv
    scaled = gn * gain_ref[...]
    gh = inv * (scaled - normed * jnp.mean(scaled * normed, -1, keepdims=True))
    hid_s[...] = gh
    ghb = gh.astype(BF)
    bext[HALO : HALO + ROWS, :] = ghb

    wide = ghb.astype(F32)
    for b in range(CHIPS):
        turned = wide if b == 0 else pltpu.roll(wide, CH - 96 * b, 1)
        bst[b] = turned[:, :HD].astype(BF)

    def b_copy(chip, dev):
        return rcopy(bst.at[chip], bh.at[slot], bs.at[chip], br.at[slot], dev)

    def b_local(chip):
        bh[slot] = bst[chip]

    to_worker(b_copy, b_local)

    up = rcopy(bext.at[ROWS : ROWS + HALO], bext.at[0:HALO], h2s.at[0], h2r.at[0], {"seq": (j + 1) % SEQ})
    down = rcopy(
        bext.at[HALO : 2 * HALO], bext.at[HALO + ROWS :], h2s.at[1], h2r.at[1], {"seq": (j + SEQ - 1) % SEQ}
    )
    pl.when(j < SEQ - 1)(lambda: up.start())
    pl.when(j > 0)(lambda: down.start())

    @pl.when(j == 0)
    def _():
        bext[0:HALO, :] = jnp.zeros((HALO, CH), BF)

    @pl.when(j == SEQ - 1)
    def _():
        bext[HALO + ROWS :, :] = jnp.zeros((HALO, CH), BF)

    def take(buf, ss, rs):
        def step(i):
            frm = (d + 1 + i) % DP
            rcopy(buf.at[frm], buf.at[frm], ss.at[frm], rs.at[frm], {"dp": frm}).wait_recv()

        loop(15, step)
        total = buf[0].astype(F32)
        for i in range(1, DP):
            total = total + buf[i].astype(F32)
        return total.astype(BF)

    mine = jnp.maximum(15 - d, 0)
    unit = SEQ * (mine // 4) + j
    owner = unit // 3
    row = (unit % 3) * 4 + mine % 4

    def red_copy(i):
        to = (d + i) % DP
        return rcopy(red, gfin.at[row], gus.at[to], gur.at[row], {"dp": to, "seq": owner})

    @pl.when(d >= 4)
    def _():
        rq[d] = gown[15 - d]
        red[...] = take(rq, rqs, rqr)
        loop(15, lambda i: red_copy(i + 1).start())
        pl.when(owner != j)(lambda: red_copy(0).start())

        @pl.when(owner == j)
        def _():
            gfin[row] = red[...]

    def b_wait(b):
        wait_slot(bh, bs, br, b)

    loop(CHIPS, b_wait)
    bt[...] = flip(bh[...].reshape(HALF, HD))[:96].astype(BF)

    def cp_copy(n):
        return rcopy(cst.at[n], crcv.at[n], cps.at[n], cpr.at[n], mate)

    for n in range(2):
        for t in range(TAPS):
            rows = slice(t * GAP, t * GAP + HALF)
            cg[n, t * 96 : t * 96 + 96, :] = dot(bt[...], ag[rows, n * PART : (n + 1) * PART])
        for t in range(TAPS):
            rows = pl.ds(pl.multiple_of(t * 96 + (1 - k) * 48, 48), 48)
            cst[n, t * 3 : t * 3 + 3] = cg[n, rows, :].astype(BF).reshape(3, 16, PART)
        cp_copy(n).start()

    def rc_copy(n, to):
        return rcopy(
            ct.at[n, jnp.minimum(to, 14)], rc.at[n, d], rcs.at[n, to], rcr.at[n, d], {"dp": to}
        )

    for n in range(2):
        cp_copy(n).wait_recv()
        for t in range(TAPS):
            rows = pl.ds(pl.multiple_of(t * 96 + k * 48, 48), 48)
            own = cg[n, rows, :].reshape(3, 16, PART)
            ct[n, t * 3 : t * 3 + 3] = (own + crcv[n, t * 3 : t * 3 + 3].astype(F32)).astype(BF)

        def rc_send(i, n=n):
            to = (d + 1 + i) % DP
            pl.when(to < 15)(lambda: rc_copy(n, to).start())

        loop(15, rc_send)

    pl.when(j > 0)(lambda: up.wait_recv())
    pl.when(j < SEQ - 1)(lambda: down.wait_recv())
    ga = jnp.zeros((ROWS, CH), F32)
    for t in range(TAPS):
        lo = (TAPS - 1 - t) * GAP
        ga = ga + dot_nt(bext[lo : lo + ROWS, :], cwv[t])
    x = x_ref[...].astype(F32)
    th = gelu_tanh(x)
    slope = 0.5 * (1.0 + th) + 0.5 * x * (1.0 - th * th) * GELU_A * (1.0 + 3.0 * GELU_B * x * x)
    gi_ref[...] = (hid_s[...] + slope * ga).astype(BF)

    def fc_copy(n, m, to):
        return rcopy(cfin.at[n, m], cfin.at[n, m], fcs.at[n, to], fcr.at[n, m], {"dp": to})

    @pl.when(d < 15)
    def _():
        for n in range(2):
            rc[n, d] = ct[n, d]
            cfin[n, d] = take(rc.at[n], rcs.at[n], rcr.at[n])
            loop(15, lambda i, n=n: fc_copy(n, d, (d + 1 + i) % DP).start())

    def o_wait(chip):
        @pl.when(2 * chip + home != j)
        def _():
            lanes = pl.ds(pl.multiple_of(chip * HD, HD), HD)
            rcopy(obuf.at[0], att_ref.at[:, lanes], os_.at[0], or_.at[chip], mate).wait_recv()

    loop(CHIPS, o_wait)

    for r in range(3):
        u = 3 * j + r
        for q in range(4):
            frm = u % SEQ
            at = 15 - (4 * (u // SEQ) + q)

            @pl.when((frm != j) | (at != d))
            def _(row=r * 4 + q):
                rcopy(red, gfin.at[row], gus.at[0], gur.at[row], mate).wait_recv()

    for n in range(2):
        def land_c(i, n=n):
            frm = (d + 1 + i) % DP
            pl.when(frm < 15)(lambda: fc_copy(n, frm, frm).wait_recv())

        loop(15, land_c)

    for g in range(GROUPS):
        to_worker_done(x_copy(g))
    to_worker_done(do_copy)
    to_worker_done(b_copy)

    @pl.when((j == 7) | (j == 8))
    def _():
        def step(chip):
            pl.when(chip != c)(lambda: xh_copy(chip).wait_send())

        loop(CHIPS, step)

    pl.when(k == c // 4)(lambda: hd_copy.wait_send())

    def mates(p):
        kv_copy(p).wait_send()
        pr_copy(p).wait_send()

    loop(TILES, mates)

    def given(b):
        @pl.when(owner_of(b) != j)
        def _():
            o_copy(b).wait_send()
            kv_back(b).wait_send()
            dq_copy(b).wait_send()

    loop(CHIPS, given)
    gp_copy.wait_send()

    @pl.when(d >= 4)
    def _():
        loop(15, lambda i: red_copy(i + 1).wait_send())
        pl.when(owner != j)(lambda: red_copy(0).wait_send())

    pl.when(j < SEQ - 1)(lambda: up.wait_send())
    pl.when(j > 0)(lambda: down.wait_send())
    for n in range(2):
        cp_copy(n).wait_send()

    def drain(i):
        to = (d + 1 + i) % DP
        pl.when(to >= 4)(lambda: rq_copy(to).wait_send())
        for n in range(2):
            pl.when(to < 15)(lambda n=n: rc_copy(n, to).wait_send())
            pl.when(d < 15)(lambda n=n: fc_copy(n, 0, to).wait_send())

    loop(15, drain)


def finish(att_ref, gi_ref, cfin, gfin, att_out, gi_out, cw_out, w_out, cbuf, gbuf, sem):
    copies = [pltpu.make_async_copy(att_ref, att_out, sem.at[0]), pltpu.make_async_copy(gi_ref, gi_out, sem.at[1])]
    for cp in copies:
        cp.start()
    gbuf[...] = gfin[...].astype(F32).reshape(192, CH).T
    copies.append(pltpu.make_async_copy(gbuf, w_out, sem.at[2]))
    copies[-1].start()
    for t in range(TAPS):
        for n in range(2):
            rows = cfin[n, t * 3 : t * 3 + 3].astype(F32).reshape(48, PART)
            cbuf[t, n * PART : (n + 1) * PART, :] = rows.T
    copies.append(pltpu.make_async_copy(cbuf, cw_out, sem.at[3]))
    copies[-1].start()
    for cp in copies:
        cp.wait()


def body(inputs, convolution_weight, w_qkv, gain, out_grad):
    vm = pl.BlockSpec(memory_space=pltpu.VMEM)
    hbm = pl.BlockSpec(memory_space=pl.ANY)
    V = pltpu.VMEM

    def sem(*n):
        return pltpu.SemaphoreType.DMA(n)

    scratch = [
        V((TAPS, CH, CH), BF),
        V((CH, 3 * INNER), BF),
        V((CH, 3 * HD), BF),
        V((GROUPS, CHIPS, ROWS, WIDE), BF),
        V((HALO, CH), BF),
        V((HALF + 2 * HALO, CH), BF),
        V((TILES, TILE, CH), F32),
        V((2, ROWS, CH), F32),
        V((ROWS, CH), F32),
        V((TILES, TILE, CH), BF),
        V((CHIPS, ROWS, HD), BF),
        V((TILES, HD, TILE), BF),
        V((HALF, HD), BF),
        V((TILES, HD, TILE), BF),
        V((2, TILES, TILE, 2 * HD), BF),
        V((2 * TILES, HD, TILE), BF),
        V((2 * TILES, HD, TILE), BF),
        V((2 * TILES, TILE, HALF), BF),
        V((2, 8, HALF), F32),
        V((HALF, HD), BF),
        V((HD, HALF), F32),
        V((TILES, 2, TILE, HD), F32),
        V((TILES, 2, TILE, HD), F32),
        V((CHIPS, ROWS, HD), BF),
        V((CHIPS, ROWS, HD), BF),
        V((2, CHIPS, ROWS, HD), BF),
        V((TILES, 3 * HD, TILE), BF),
        V((3, ROWS, INNER), BF),
        V((3 * HD, CH), F32),
        V((12, 16, CH), BF),
        V((12, 16, CH), BF),
        V((12, 16, CH), BF),
        V((DP, 16, CH), BF),
        V((16, CH), BF),
        V((ROWS + 2 * HALO, CH), BF),
        V((CHIPS, ROWS, HD), BF),
        V((CHIPS, ROWS, HD), BF),
        V((96, HALF), BF),
        V((2, TAPS * 96, PART), F32),
        V((2, 15, 16, PART), BF),
        V((2, 15, 16, PART), BF),
        V((2, 15, 16, PART), BF),
        V((2, DP, 16, PART), BF),
        sem(9),
        sem(3, 8), sem(3, 8), sem(8), sem(1), sem(8), sem(8), sem(1), sem(1),
        sem(4), sem(4), sem(8), sem(8), sem(8), sem(8), sem(8), sem(8), sem(4), sem(4),
        sem(1), sem(1), sem(16), sem(16), sem(16), sem(12),
        sem(2), sem(2), sem(8), sem(8), sem(2), sem(2),
        sem(2, 16), sem(2, 16), sem(2, 16), sem(2, 15),
    ]
    att, gi, cfin, gfin = pl.pallas_call(
        kernel,
        out_shape=[
            jax.ShapeDtypeStruct((ROWS, INNER), BF),
            jax.ShapeDtypeStruct((ROWS, CH), BF),
            jax.ShapeDtypeStruct((2, 15, 16, PART), BF),
            jax.ShapeDtypeStruct((12, 16, CH), BF),
        ],
        in_specs=[vm, vm, vm, hbm, hbm],
        out_specs=[vm, vm, vm, vm],
        scratch_shapes=scratch,
        compiler_params=pltpu.CompilerParams(
            collective_id=0, has_side_effects=True, vmem_limit_bytes=58 * 1024 * 1024
        ),
        cost_estimate=pl.CostEstimate(flops=14_000_000_000, bytes_accessed=15_000_000, transcendentals=3_000_000),
    )(inputs[0], gain.reshape(1, CH), out_grad[0], convolution_weight, w_qkv)
    att, gi, conv, qkv = pl.pallas_call(
        finish,
        out_shape=[
            jax.ShapeDtypeStruct((ROWS, INNER), BF),
            jax.ShapeDtypeStruct((ROWS, CH), BF),
            jax.ShapeDtypeStruct((TAPS, CH, 48), F32),
            jax.ShapeDtypeStruct((CH, 192), F32),
        ],
        in_specs=[vm, vm, vm, vm],
        out_specs=[hbm, hbm, hbm, hbm],
        scratch_shapes=[V((TAPS, CH, 48), F32), V((CH, 192), F32), sem(4)],
    )(att, gi, cfin, gfin)
    return att[None], gi[None], conv, qkv


def solution(mesh):
    in_specs = (P("dp", "seq", None), P(), P(), P(), P("dp", "seq", None))
    out_specs = (P("dp", "seq", None), P("dp", "seq", None), P(None, None, "seq"), P(None, "seq"))
    return jax.shard_map(body, mesh=mesh, in_specs=in_specs, out_specs=out_specs, check_vma=False)
```

time: 472 us -> 112 us (0.24)
  the two profiles are of different devices: /device:TPU:6 before, /device:TPU:1 now
where the time goes in v2:
time: 112 us
  Pallas kernels  105 us (94%)
  local copies, waits for them, and re-layouts  6.43 us (6%)
    pallas_call x1, Pallas kernels, body(): pl.pallas_call(kernel, out_shape=[jax.ShapeDtypeStruct((ROWS, INNER), BF)...  102 us
    unnamed x2, local copies, waits for them, and re-layouts  5.16 us
    pallas_call x1, Pallas kernels, body(): pl.pallas_call(finish, out_shape=[jax.ShapeDtypeStruct((ROWS, INNER), BF)...  3.03 us

profile of v2, /device:TPU:1, one launch (start us, length us, event | category | flops | bytes accessed | tf_op | source)
XLA Modules:
  0.0 112.2 jit_solution(15579961963967673424)
XLA Ops:
  0.6 1.3 %reshape.11.gain_ref = f32[1,768]{1,0:T(1,128)} reshape(f32[768]{0:T(1024)} %param.8) | data formatting | bytes 6144 | tf_op jit(solution)/shard_map/reshape | solution.py:700
  1.9 102.1 %shard_map.84 = (bf16[128,1024]{1,0:T(8,128)(2,1)}, bf16[128,768]{1,0:T(8,128)(2,1)}, bf16[2,15,16,384]{3,2,1,0:T(8,128)(2,1)}, bf16[12,16,768]{2,1,0:T(8,128)(2,1)}) custom-call(bf16[128,768]{1,0:T(8,128)(2,1)} %bitcast.6, f32[1,768]{1,0:T(1,128)} %reshape.11.gain_ref, bf16[128,1024]{1,0:T(8,128)(2,1)} %bitcast.4, bf16[5,768,768]{2,1,0:T(8,128)(2,1)} %cw_hbm.1, ...), custom_call_target="tpu_custom_call" | custom-call | flops 14000000000 | bytes 15000000 | tf_op jit(solution)/shard_map/pallas_call | solution.py:685
  104.0 3.0 %shard_map.85 = (bf16[128,1024]{1,0:T(8,128)(2,1)}, bf16[128,768]{1,0:T(8,128)(2,1)}, f32[5,768,48]{2,1,0:T(8,128)}, f32[768,192]{1,0:T(8,128)}) custom-call(bf16[128,1024]{1,0:T(8,128)(2,1)} %get-tuple-element.12.att_ref, bf16[128,768]{1,0:T(8,128)(2,1)} %get-tuple-element.13.gi_ref, bf16[2,15,16,384]{3,2,1,0:T(8,128)(2,1)} %get-tuple-element.14.cfin, ...), custom_call_target="tpu_custom_call" | custom-call | tf_op jit(solution)/shard_map/pallas_call | solution.py:701
  107.0 2.2 %copy.10 = f32[768,192]{0,1:T(8,128)} copy(f32[768,192]{1,0:T(8,128)} %get-tuple-element.23) | data formatting | bytes 1179648
  109.2 3.0 %copy.9 = f32[5,768,48]{1,2,0:T(8,128)} copy(f32[5,768,48]{2,1,0:T(8,128)} %get-tuple-element.22) | data formatting | bytes 1474560

commit v3 on v2

v3 whole, which is shorter than its diff:
```python
import jax
import jax.numpy as jnp
from jax import lax
from jax.experimental import pallas as pl
from jax.experimental.pallas import tpu as pltpu
from jax.sharding import PartitionSpec as P

CH = 768
HEADS = 8
HD = 128
INNER = HEADS * HD
TAPS = 5
GAP = 16
HALO = 32
PAD = 2 * HALO
ROWS = 128
SEQ = 16
DP = 16
ZS = 8
CHIPS = 8
HALF = CHIPS * ROWS
TILE = 256
TILES = HALF // TILE
PART = 384
GROUPS = 3
WIDE = CH // GROUPS
TEMPER = HD ** (-0.5)
LOG2E = 1.4426950408889634
GELU_A = 0.7978845608028654
GELU_B = 0.044715
BF = jnp.bfloat16
F32 = jnp.float32
MESH = pl.DeviceIdType.MESH


def rcopy(src, dst, ss, rs, dev):
    return pltpu.make_async_remote_copy(
        src_ref=src, dst_ref=dst, send_sem=ss, recv_sem=rs, device_id=dev, device_id_type=MESH
    )


def dot(a, b):
    return jnp.dot(a, b, preferred_element_type=F32)


def dot_nt(a, b):
    return lax.dot_general(a, b, (((1,), (1,)), ((), ())), preferred_element_type=F32)


def flip(a):
    return a.astype(F32).T


def gelu_tanh(x):
    return jnp.tanh(GELU_A * (x + GELU_B * x * x * x))


def gelu(x):
    x = x.astype(F32)
    return (0.5 * x * (1.0 + gelu_tanh(x))).astype(BF)


def loop(n, step):
    lax.fori_loop(0, n, lambda i, carry: (step(i), carry)[1], 0)


def kernel(
    x_hbm, gain_hbm, og_hbm, cw_hbm, w_hbm,
    att_ref, gi_ref, cfin, gfin,
    x_ref, gain_ref, og_ref, cwv, wfull, wh, xg, ag, apad, epad, acc_s, gn_s, hid_s, nh, doh, dot_s, qd, qt_s, kv, vt_s,
    wts, stat_s, ot_s, dor_s, dqt, dkvp, pr, obuf, dqb, gsrc, gt, res, gtf, gst, grcv, gown,
    rq, redp, redr, red, bext, bst, bh, bt, cg, cst, crcv, give_c, keep_c, px, zs, rc,
    wsem, xs, xr, xps, xhs, xhr, dos, dor, hds, hdr, kvs, kvr, os_, or_, dqs, dqr, ks, kr, prs, prr,
    gps, gpr, rqs, rqr, rps, rpr, gus, gur, h2s, h2r, bs, br, cps, cpr,
    pxs, pxr, rcs, rcr, fzs, fzr,
):
    j = lax.axis_index("seq")
    d = lax.axis_index("dp")
    c = j // 2
    k = j % 2
    mate = {"seq": j + 1 - 2 * k}
    home = j // CHIPS
    slot = j % CHIPS
    col = pl.multiple_of(c * HD, HD)

    barrier = pltpu.get_barrier_semaphore()

    def hello(i):
        pl.semaphore_signal(barrier, inc=1, device_id={"seq": (j + i + 1) % SEQ}, device_id_type=MESH)
        pl.semaphore_signal(barrier, inc=1, device_id={"dp": (d + i + 1) % DP}, device_id_type=MESH)

    loop(15, hello)
    x_in = pltpu.make_async_copy(x_hbm, x_ref, wsem.at[9])
    og_in = pltpu.make_async_copy(og_hbm, og_ref, wsem.at[10])
    gain_in = pltpu.make_async_copy(gain_hbm, gain_ref, wsem.at[11])
    x_in.start()
    og_in.start()
    gain_in.start()
    for t in range(TAPS):
        pltpu.make_async_copy(cw_hbm.at[t], cwv.at[t], wsem.at[t]).start()
    for p in range(3):
        pltpu.make_async_copy(
            w_hbm.at[:, pl.ds(p * INNER + col, HD)], wh.at[:, pl.ds(p * HD, HD)], wsem.at[5 + p]
        ).start()
    wf_copy = pltpu.make_async_copy(w_hbm, wfull, wsem.at[8])
    wf_copy.start()

    dqt[...] = jnp.zeros_like(dqt)
    acc_s[...] = jnp.zeros_like(acc_s)
    for p in range(TILES):
        apad[p, :PAD, :] = jnp.zeros((PAD, CH), BF)
        apad[p, PAD + TILE :, :] = jnp.zeros((PAD, CH), BF)
    epad[:PAD, :] = jnp.zeros((PAD, CH), BF)
    epad[PAD + HALO :, :] = jnp.zeros((PAD, CH), BF)

    @pl.when(k == 0)
    def _():
        ag[0:HALO, :] = jnp.zeros((HALO, CH), BF)

    @pl.when(k == 1)
    def _():
        ag[HALO + HALF :, :] = jnp.zeros((HALO, CH), BF)

    pl.semaphore_wait(barrier, 30)

    def to_worker(copy, local):
        def step(i):
            chip = (c + CHIPS - 1 - i) % CHIPS
            dev = 2 * chip + home

            @pl.when(dev != j)
            def _():
                copy(chip, {"seq": dev}).start()

            if local is not None:
                pl.when(dev == j)(lambda: local(chip))

        loop(CHIPS, step)

    def to_worker_done(copy):
        def step(chip):
            dev = 2 * chip + home

            @pl.when(dev != j)
            def _():
                copy(chip, {"seq": dev}).wait_send()

        loop(CHIPS, step)

    def owner_of(b):
        return CHIPS * k + b

    flip_x = c + 1 - 2 * (c % 2)
    near = (flip_x, (c + 2) % CHIPS, (c + 6) % CHIPS, (c + 4) % CHIPS, c)

    def x_copy(g, i):
        src = x_ref.at[:, g * WIDE : (g + 1) * WIDE]
        return rcopy(src, xg.at[g, slot], xs.at[g, i], xr.at[g, slot], {"seq": 2 * near[i] + home})

    def x_left(g):
        for i in range(4):
            x_copy(g, i).wait_send()

    def send_x(g):
        for i in range(4):
            x_copy(g, i).start()
        pl.when(home != k)(lambda: x_copy(g, 4).start())

        @pl.when(home == k)
        def _():
            xg[g, slot] = x_ref[:, g * WIDE : (g + 1) * WIDE]

    x_in.wait()
    send_x(0)
    x_left(0)
    send_x(1)

    inside = c // 4 == k
    passed = jnp.where(inside, flip_x, (c + 4) % CHIPS) - 4 * k

    def pass_copy(g, e, chip, i):
        b = 2 * passed + e
        return rcopy(xg.at[g, b], xg.at[g, b], xps.at[g, e, i], xr.at[g, b], {"seq": 2 * chip + k})

    def hand_on(g, e):
        b = 2 * passed + e
        rcopy(xg.at[g, b], xg.at[g, b], xps.at[g, e, 0], xr.at[g, b], mate).wait_recv()

        @pl.when(inside)
        def _():
            pass_copy(g, e, near[1], 0).start()
            pass_copy(g, e, near[2], 1).start()

        pl.when(c // 4 != k)(lambda: pass_copy(g, e, flip_x, 0).start())

    def relay(g):
        hand_on(g, 0)
        hand_on(g, 1)

    def wait_slot(buf, ss, rs, b):
        @pl.when(owner_of(b) != j)
        def _():
            rcopy(buf.at[b], buf.at[b], ss.at[0], rs.at[b], mate).wait_recv()

    def kv_copy(p):
        return rcopy(kv.at[k, p], kv.at[k, p], kvs.at[p], kvr.at[p], mate)

    def do_copy(chip, dev):
        src = og_ref.at[:, pl.ds(pl.multiple_of(chip * HD, HD), HD)]
        return rcopy(src, doh.at[slot], dos.at[chip], dor.at[slot], dev)

    def do_local(chip):
        doh[slot] = og_ref[:, pl.ds(pl.multiple_of(chip * HD, HD), HD)]

    edge_copy = rcopy(
        apad.at[3 - 3 * k, pl.ds(pl.multiple_of(PAD + (TILE - HALO) * (1 - k), HALO), HALO)],
        epad.at[pl.ds(PAD, HALO)], xhs.at[0], xhr.at[0], mate,
    )
    def unit(g, direct):
        lanes = slice(g * WIDE, (g + 1) * WIDE)
        low = c % 2 if direct else 1 - c % 2
        for q in range(2):
            p = low + 2 * q
            for e in range(2):
                b = 2 * p + e

                @pl.when((owner_of(b) != j) & (p != passed))
                def _(b=b):
                    rcopy(xg.at[g, b], xg.at[g, b], xps.at[g, 0, 0], xr.at[g, b], mate).wait_recv()

            rows = gelu(xg[g, pl.ds(2 * p, 2)].reshape(TILE, WIDE))
            apad[p, PAD : PAD + TILE, lanes] = rows
            ag[pl.ds(pl.multiple_of(HALO + p * TILE, HALO), TILE), lanes] = rows
        if g == GROUPS - 1 and not direct:
            edge_copy.start()
        weights = cwv[:, lanes, :].reshape(TAPS * WIDE, CH)
        for q in range(2):
            p = low + 2 * q
            windows = [apad[p, t * GAP : t * GAP + TILE + PAD, lanes] for t in range(TAPS)]
            rows = pl.ds(pl.multiple_of(p * TILE, TILE), TILE + PAD)
            acc_s[rows, :] = acc_s[rows, :] + dot(jnp.concatenate(windows, axis=1), weights)

    for t in range(TAPS):
        pltpu.make_async_copy(cw_hbm.at[t], cwv.at[t], wsem.at[t]).wait()
    relay(0)
    unit(0, True)
    x_left(1)
    send_x(2)
    relay(1)
    unit(1, True)
    unit(0, False)
    relay(2)
    og_in.wait()
    to_worker(do_copy, do_local)
    unit(2, True)
    unit(1, False)
    gain_in.wait()
    unit(2, False)

    for p in range(3):
        pltpu.make_async_copy(
            w_hbm.at[:, pl.ds(p * INNER + col, HD)], wh.at[:, pl.ds(p * HD, HD)], wsem.at[5 + p]
        ).wait()

    def finish_rows(p):
        rows = pl.ds(pl.multiple_of(HALO + p * 2 * TILE, HALO), 2 * TILE)
        x = jnp.concatenate([xg[g, pl.ds(4 * p, 4)].reshape(2 * TILE, WIDE) for g in range(GROUPS)], axis=1)
        acc = acc_s[rows, :] + x.astype(F32)
        acc_s[rows, :] = acc
        inv = lax.rsqrt(jnp.mean(acc * acc, -1, keepdims=True) + 1e-6)
        rows_bf = (acc * inv * gain_ref[...].reshape(1, CH)).astype(BF)
        nh[pl.ds(2 * p, 2)] = rows_bf.reshape(2, TILE, CH)
        outb = dot(rows_bf, wh[...]).astype(BF)
        kv[k, pl.ds(2 * p, 2)] = outb[:, HD:].reshape(2, TILE, 2 * HD)
        qd[pl.ds(pl.multiple_of(p * 2 * TILE, TILE), 2 * TILE), :] = outb[:, :HD]
        for e in range(2):
            qt_s[2 * p + e] = outb[e * TILE : (e + 1) * TILE, :HD].T
            vt_s[k * TILES + 2 * p + e] = outb[e * TILE : (e + 1) * TILE, 2 * HD :].T
        kv_copy(2 * p).start()
        kv_copy(2 * p + 1).start()

    finish_rows(k)
    edge_copy.wait_recv()
    ag[pl.ds(pl.multiple_of((HALF + HALO) * (1 - k), HALO), HALO), :] = epad[PAD : PAD + HALO, :]
    windows = [epad[pl.ds(pl.multiple_of((3 + k + q) * GAP, GAP), HALO), :] for q in range(2)]
    part = dot(jnp.concatenate(windows, axis=1), cwv[pl.ds(3 - 3 * k, 2)].reshape(2 * CH, CH))
    rows = pl.ds(pl.multiple_of(HALF - (HALF - HALO) * k, HALO), HALO)
    acc_s[rows, :] = acc_s[rows, :] + part
    finish_rows(1 - k)

    def hidden_rows(core):
        return acc_s.at[pl.ds(pl.multiple_of(HALO + (c % 4) * TILE + core * ROWS, HALO), ROWS)]

    hd_copy = rcopy(hidden_rows(1 - k), hid_s, hds.at[0], hdr.at[0], mate)

    @pl.when(k == c // 4)
    def _():
        hd_copy.start()
        hid_s[...] = hidden_rows(k)[...]

    def other_keys(p):
        rcopy(kv.at[1 - k, p], kv.at[1 - k, p], kvs.at[p], kvr.at[p], mate).wait_recv()
        vt_s[(1 - k) * TILES + p] = kv[1 - k, p, :, HD:].T

    loop(TILES, other_keys)

    def give(copy, local, p):
        for e in range(2):
            b = 2 * p + e
            pl.when(owner_of(b) != j)(lambda b=b: copy(b).start())
            pl.when(owner_of(b) == j)(lambda b=b: local(b))

    def o_copy(b):
        return rcopy(
            obuf.at[b], att_ref.at[:, pl.ds(col, HD)], os_.at[b], or_.at[c], {"seq": owner_of(b)}
        )

    def o_local(b):
        att_ref[:, pl.ds(col, HD)] = obuf[b]

    def forward(t):
        qt = qt_s[t]
        top = None
        for i in range(2 * TILES):
            s = dot(kv[i // TILES, i % TILES, :, :HD], qt)
            part = jnp.max(s.reshape(TILE // 8, 8, TILE), axis=0)
            top = part if top is None else jnp.maximum(top, part)
        top = jnp.max(top, axis=0, keepdims=True) * (TEMPER * LOG2E)
        total = jnp.zeros((8, TILE), F32)
        ot = jnp.zeros((HD, TILE), F32)
        lanes = pl.ds(pl.multiple_of(t * TILE, TILE), TILE)
        for i in range(2 * TILES):
            s = dot(kv[i // TILES, i % TILES, :, :HD], qt)
            p = jnp.exp2(s * (TEMPER * LOG2E) - top)
            total = total + jnp.sum(p.reshape(TILE // 8, 8, TILE), axis=0)
            pb = p.astype(BF)
            wts[i, :, lanes] = pb
            ot = ot + dot(vt_s[i], pb)
        rec = 1.0 / jnp.sum(total, axis=0, keepdims=True)
        otb = (ot * rec).astype(BF)
        ot_s[t] = otb
        stat_s[0, :, lanes] = jnp.broadcast_to(rec, (8, TILE))
        obuf[pl.ds(2 * t, 2)] = otb.T.reshape(2, ROWS, HD)

    def turn(i, core):
        return (c + i + core) % TILES

    def forward_two(i):
        forward(turn(2 * i, k))
        forward(turn(2 * i + 1, k))
        give(o_copy, o_local, turn(2 * i, k))
        give(o_copy, o_local, turn(2 * i + 1, k))

    loop(TILES // 2, forward_two)

    loop(CHIPS, lambda b: wait_slot(doh, dos, dor, b))
    for t in range(TILES):
        lanes = slice(t * TILE, (t + 1) * TILE)
        got = doh[2 * t : 2 * t + 2].reshape(TILE, HD).T
        dot_s[t] = got
        go = got.astype(F32)
        dots = jnp.sum(go * ot_s[t].astype(F32), axis=0, keepdims=True)
        stat_s[1, :, lanes] = jnp.broadcast_to(dots, (8, TILE))
        dor_s[lanes, :] = (go * stat_s[0, 0:1, lanes]).T.astype(BF)

    def backward(h, m):
        g = h * TILES + m
        vc = kv[h, m, :, HD:]
        w = wts[g]
        parts = []
        for t in range(TILES):
            lanes = slice(t * TILE, (t + 1) * TILE)
            gw = dot(vc, dot_s[t])
            slope = (gw - stat_s[1, 0:1, lanes]) * stat_s[0, 0:1, lanes]
            parts.append((w[:, lanes].astype(F32) * slope).astype(BF))
        ds = jnp.concatenate(parts, axis=1)
        dv = dot(w, dor_s[...])
        dk = dot(ds, qd[...])
        dqt[...] = dqt[...] + dot(kv[h, m, :, :HD].T, ds)
        return dk * TEMPER, dv

    def pr_copy(m):
        return rcopy(dkvp.at[m], pr.at[m], prs.at[m], prr.at[m], mate)

    early = turn(0, 1 - k)
    dk, dv = backward(1 - k, early)
    dkvp[early, 0] = dk
    dkvp[early, 1] = dv
    pr_copy(early).start()

    def kv_back(b):
        return rcopy(
            gsrc.at[b], res.at[c, 1:3], ks.at[b], kr.at[c], {"seq": owner_of(b)}
        )

    def kv_local(b):
        res[c, 1:3] = gsrc[b]

    def halves(i):
        m = turn(i, k)
        ahead = turn(i + 1, 1 - k)

        @pl.when(i < TILES - 1)
        def _():
            dk, dv = backward(1 - k, ahead)
            dkvp[ahead, 0] = dk
            dkvp[ahead, 1] = dv
            pr_copy(ahead).start()

        dk, dv = backward(k, m)
        pr_copy(m).wait_recv()
        dk = dk + pr[m, 0]
        dv = dv + pr[m, 1]
        for e in range(2):
            gsrc[2 * m + e, 0] = dk[e * ROWS : (e + 1) * ROWS].astype(BF)
            gsrc[2 * m + e, 1] = dv[e * ROWS : (e + 1) * ROWS].astype(BF)
        give(kv_back, kv_local, m)
        gt[m, HD : 2 * HD, :] = dk.T.astype(BF)
        gt[m, 2 * HD :, :] = dv.T.astype(BF)

    loop(TILES, halves)

    def dq_copy(b):
        return rcopy(
            dqb.at[b], res.at[c, 0], dqs.at[b], dqr.at[c], {"seq": owner_of(b)}
        )

    def dq_local(b):
        res[c, 0] = dqb[b]

    def query_back(i):
        t = turn(i, k)
        dq = dqt[:, pl.ds(pl.multiple_of(t * TILE, TILE), TILE)] * TEMPER
        dqb[pl.ds(2 * t, 2)] = dq.T.astype(BF).reshape(2, ROWS, HD)
        give(dq_copy, dq_local, t)
        gt[t, :HD, :] = dq.astype(BF)

    loop(TILES, query_back)

    gtf[...] = dot(jnp.concatenate([gt[t] for t in range(TILES)], axis=1), nh[...].reshape(HALF, CH))
    for p in range(3):
        rows = pl.ds(pl.multiple_of(p * HD + (1 - k) * 64, 64), 64)
        gst[p * 4 : p * 4 + 4] = gtf[rows, :].astype(BF).reshape(4, 16, CH)
    gp_copy = rcopy(gst, grcv, gps.at[0], gpr.at[0], mate)
    gp_copy.start()
    gp_copy.wait_recv()
    for p in range(3):
        rows = pl.ds(pl.multiple_of(p * HD + k * 64, 64), 64)
        own = gtf[rows, :].reshape(4, 16, CH)
        both = own + grcv[p * 4 : p * 4 + 4].astype(F32)
        for h in range(2):
            gown[8 * p + 4 * h : 8 * p + 4 * h + 4] = both[:, :, h * PART : (h + 1) * PART].astype(BF)

    z = d // 2
    xl = d % 2
    partner = {"dp": d + 1 - 2 * xl}

    def ring(off):
        zz = (z + off) % ZS
        return zz, {"dp": 2 * zz + xl}

    FAR = (4, 3, 5, 2, 6, 1, 7)

    def rq_copy(off):
        zz, dev = ring(off)
        return rcopy(gown.at[pl.ds(3 * zz, 3)], rq.at[z], rqs.at[zz], rqr.at[z], dev)

    for off in FAR:
        rq_copy(off).start()

    def back(copy):
        def step(i):
            chip = (c + i) % CHIPS
            pl.when(2 * chip + home != j)(lambda: copy(chip).wait_recv())

        loop(CHIPS, step)

    @pl.when(k != c // 4)
    def _():
        hd_copy.wait_recv()

    wf_copy.wait()

    def heads(i):
        return jnp.concatenate([res[h, i] for h in range(HEADS)], axis=1)

    back(lambda chip: rcopy(gsrc.at[0], res.at[chip, 1:3], ks.at[0], kr.at[chip], mate))
    gn_s[...] = dot_nt(jnp.concatenate([heads(1), heads(2)], axis=1), wfull[:, INNER:])
    back(lambda chip: rcopy(dqb.at[0], res.at[chip, 0], dqs.at[0], dqr.at[chip], mate))
    gn = gn_s[...] + dot_nt(heads(0), wfull[:, :INNER])
    hidden = hid_s[...]
    inv = lax.rsqrt(jnp.mean(hidden * hidden, -1, keepdims=True) + 1e-6)
    normed = hidden * inv
    scaled = gn * gain_ref[...].reshape(1, CH)
    gh = inv * (scaled - normed * jnp.mean(scaled * normed, -1, keepdims=True))
    hid_s[...] = gh
    ghb = gh.astype(BF)
    bext[HALO : HALO + ROWS, :] = ghb

    bst[...] = gh.T.astype(BF).reshape(CHIPS, 96, ROWS)

    def b_copy(chip, dev):
        return rcopy(bst.at[chip], bh.at[slot], bs.at[chip], br.at[slot], dev)

    def b_local(chip):
        bh[slot] = bst[chip]

    to_worker(b_copy, b_local)

    class Edges:
        def __init__(self, buf, ss, rs):
            self.up = rcopy(
                buf.at[ROWS : ROWS + HALO], buf.at[0:HALO], ss.at[0], rs.at[0], {"seq": (j + 1) % SEQ}
            )
            self.down = rcopy(
                buf.at[HALO : 2 * HALO], buf.at[HALO + ROWS :], ss.at[1], rs.at[1], {"seq": (j + SEQ - 1) % SEQ}
            )

        def start(self):
            pl.when(j < SEQ - 1)(lambda: self.up.start())
            pl.when(j > 0)(lambda: self.down.start())

        def wait_recv(self):
            pl.when(j > 0)(lambda: self.up.wait_recv())
            pl.when(j < SEQ - 1)(lambda: self.down.wait_recv())

        def wait_send(self):
            pl.when(j < SEQ - 1)(lambda: self.up.wait_send())
            pl.when(j > 0)(lambda: self.down.wait_send())

    edges = Edges(bext, h2s, h2r)
    edges.start()

    @pl.when(j == 0)
    def _():
        bext[0:HALO, :] = jnp.zeros((HALO, CH), BF)

    @pl.when(j == SEQ - 1)
    def _():
        bext[HALO + ROWS :, :] = jnp.zeros((HALO, CH), BF)

    def take(buf, ss, rs):
        for off in reversed(FAR):
            zz, dev = ring(off)
            rcopy(buf.at[zz], buf.at[zz], ss.at[zz], rs.at[zz], dev).wait_recv()
        total = buf[0].astype(F32)
        for i in range(1, ZS):
            total = total + buf[i].astype(F32)
        return total.astype(BF)

    rq[z] = gown[pl.ds(3 * z, 3)]
    redp[...] = take(rq, rqs, rqr)
    rp_copy = rcopy(redp, redr, rps.at[0], rpr.at[0], partner)
    rp_copy.start()

    rp_copy.wait_recv()
    red[...] = (redp[...].astype(F32) + redr[...].astype(F32)).astype(BF)

    def red_copy(i, off):
        hc = 3 * z + i
        unit = SEQ * (hc // 8) + j
        row = (unit % 3) * 8 + hc % 8
        zz = (z + off) % ZS
        dev = {"dp": 2 * zz + xl, "seq": unit // 3}
        return rcopy(red.at[i], gfin.at[row], gus.at[i, zz], gur.at[row], dev), unit // 3, row

    for i in range(3):
        for off in FAR:
            red_copy(i, off)[0].start()
        cp, owner, row = red_copy(i, 0)
        pl.when(owner != j)(cp.start)

        @pl.when(owner == j)
        def _(i=i, row=row):
            gfin[row] = red[i]

    def b_wait(b):
        wait_slot(bh, bs, br, b)

    loop(CHIPS, b_wait)
    for b in range(CHIPS):
        bt[:, b * ROWS : (b + 1) * ROWS] = bh[b]

    def cp_copy(o):
        return rcopy(cst.at[o], crcv.at[o], cps.at[o], cpr.at[o], mate)

    for o in range(2):
        n = 1 - xl if o == 0 else xl
        lanes = pl.ds(pl.multiple_of(n * PART, PART), PART)
        for t in range(TAPS):
            cg[o, t * 96 : t * 96 + 96, :] = dot(bt[...], ag[t * GAP : t * GAP + HALF, lanes])
        for t in range(TAPS):
            rows = pl.ds(pl.multiple_of(t * 96 + (1 - k) * 48, 48), 48)
            cst[o, t * 3 : t * 3 + 3] = cg[o, rows, :].astype(BF).reshape(3, 16, PART)
        cp_copy(o).start()

    give_c[15] = jnp.zeros((16, PART), BF)
    keep_c[15] = jnp.zeros((16, PART), F32)

    def with_mate(o):
        cp_copy(o).wait_recv()
        for t in range(TAPS):
            rows = pl.ds(pl.multiple_of(t * 96 + k * 48, 48), 48)
            own = cg[o, rows, :].reshape(3, 16, PART)
            both = own + crcv[o, t * 3 : t * 3 + 3].astype(F32)
            if o == 0:
                give_c[t * 3 : t * 3 + 3] = both.astype(BF)
            else:
                keep_c[t * 3 : t * 3 + 3] = both

    def px_copy(off):
        zz, _ = ring(off)
        return rcopy(give_c.at[pl.ds(2 * zz, 2)], px.at[zz], pxs.at[zz], pxr.at[zz], partner)

    with_mate(0)
    for off in FAR + (0,):
        px_copy(off).start()
    with_mate(1)

    def rc_copy(off):
        zz, dev = ring(off)
        return rcopy(zs.at[zz], rc.at[z], rcs.at[zz], rcr.at[z], dev)

    for off in FAR + (0,):
        zz, _ = ring(off)
        px_copy(off).wait_recv()
        both = (keep_c[pl.ds(2 * zz, 2)] + px[zz].astype(F32)).astype(BF)
        if off:
            zs[zz] = both
            rc_copy(off).start()
        else:
            rc[z] = both

    edges.wait_recv()
    ga = jnp.zeros((ROWS, CH), F32)
    for t in range(TAPS):
        lo = (TAPS - 1 - t) * GAP
        ga = ga + dot_nt(bext[lo : lo + ROWS, :], cwv[t])
    x = x_ref[...].astype(F32)
    th = gelu_tanh(x)
    slope = 0.5 * (1.0 + th) + 0.5 * x * (1.0 - th * th) * GELU_A * (1.0 + 3.0 * GELU_B * x * x)
    gi_ref[...] = (hid_s[...] + slope * ga).astype(BF)

    def pair(n, zz):
        return cfin.at[n, pl.ds(2 * zz, 2)]

    def fin_copy(i):
        to = (d + i) % DP
        return rcopy(pair(xl, z), pair(xl, z), fzs.at[to], fzr.at[xl, z], {"dp": to})

    cfin[xl, pl.ds(2 * z, 2)] = take(rc, rcs, rcr)
    for i in (8, 7, 9, 6, 10, 5, 11, 4, 12, 3, 13, 2, 14, 1, 15):
        fin_copy(i).start()

    def o_wait(chip):
        @pl.when(2 * chip + home != j)
        def _():
            lanes = pl.ds(pl.multiple_of(chip * HD, HD), HD)
            rcopy(obuf.at[0], att_ref.at[:, lanes], os_.at[0], or_.at[chip], mate).wait_recv()

    loop(CHIPS, o_wait)

    def land_q(row):
        u = 3 * j + row // 8
        hc = 8 * (u // SEQ) + row % 8

        @pl.when((u % SEQ != j) | (hc // 3 != z))
        def _():
            rcopy(red.at[0], gfin.at[row], gus.at[0, 0], gur.at[row], mate).wait_recv()

    loop(24, land_q)
    def land_c(i):
        n = i // ZS
        zz = i % ZS

        @pl.when((n != xl) | (zz != z))
        def _():
            rcopy(pair(n, zz), pair(n, zz), fzs.at[0], fzr.at[n, zz], partner).wait_recv()

    loop(DP, land_c)

    for g in range(GROUPS):
        if g == GROUPS - 1:
            x_left(g)
        pl.when(home != k)(lambda g=g: x_copy(g, 4).wait_send())
        for e in range(2):
            pass_copy(g, e, flip_x, 0).wait_send()
            pl.when(inside)(lambda g=g, e=e: pass_copy(g, e, flip_x, 1).wait_send())
    edge_copy.wait_send()
    to_worker_done(do_copy)
    to_worker_done(b_copy)
    pl.when(k == c // 4)(lambda: hd_copy.wait_send())
    edges.wait_send()

    def mates(p):
        kv_copy(p).wait_send()
        pr_copy(p).wait_send()

    loop(TILES, mates)

    def given(b):
        @pl.when(owner_of(b) != j)
        def _():
            o_copy(b).wait_send()
            kv_back(b).wait_send()
            dq_copy(b).wait_send()

    loop(CHIPS, given)
    gp_copy.wait_send()

    rp_copy.wait_send()
    for i in range(3):
        for off in FAR:
            red_copy(i, off)[0].wait_send()
        cp, owner, _ = red_copy(i, 0)
        pl.when(owner != j)(cp.wait_send)
    for o in range(2):
        cp_copy(o).wait_send()
    for off in FAR:
        rq_copy(off).wait_send()
        rc_copy(off).wait_send()
    for off in range(ZS):
        px_copy(off).wait_send()
    loop(15, lambda i: fin_copy(i + 1).wait_send())


def finish(att_ref, gi_ref, cfin, gfin, att_out, gi_out, cw_out, w_out, cbuf, gbuf, sem):
    copies = [pltpu.make_async_copy(att_ref, att_out, sem.at[0]), pltpu.make_async_copy(gi_ref, gi_out, sem.at[1])]
    for cp in copies:
        cp.start()
    for r in range(3):
        for h in range(2):
            piece = gfin[8 * r + 4 * h : 8 * r + 4 * h + 4].astype(F32).reshape(64, PART)
            gbuf[64 * r : 64 * r + 64, h * PART : (h + 1) * PART] = piece
    copies.append(pltpu.make_async_copy(gbuf, w_out, sem.at[2]))
    copies[-1].start()
    for n in range(2):
        cbuf[:, n * PART : (n + 1) * PART] = cfin[n, :15].astype(F32).reshape(240, PART)
    copies.append(pltpu.make_async_copy(cbuf, cw_out, sem.at[3]))
    copies[-1].start()
    for cp in copies:
        cp.wait()


def body(inputs, convolution_weight, w_qkv, gain, out_grad):
    vm = pl.BlockSpec(memory_space=pltpu.VMEM)
    hbm = pl.BlockSpec(memory_space=pl.ANY)
    V = pltpu.VMEM

    def sem(*n):
        return pltpu.SemaphoreType.DMA(n)

    scratch = [
        V((ROWS, CH), BF),
        V((CH,), F32),
        V((ROWS, INNER), BF),
        V((TAPS, CH, CH), BF),
        V((CH, 3 * INNER), BF),
        V((CH, 3 * HD), BF),
        V((GROUPS, CHIPS, ROWS, WIDE), BF),
        V((HALF + 2 * HALO, CH), BF),
        V((TILES, TILE + 2 * PAD, CH), BF),
        V((HALO + 2 * PAD, CH), BF),
        V((HALF + 2 * HALO, CH), F32),
        V((ROWS, CH), F32),
        V((ROWS, CH), F32),
        V((TILES, TILE, CH), BF),
        V((CHIPS, ROWS, HD), BF),
        V((TILES, HD, TILE), BF),
        V((HALF, HD), BF),
        V((TILES, HD, TILE), BF),
        V((2, TILES, TILE, 2 * HD), BF),
        V((2 * TILES, HD, TILE), BF),
        V((2 * TILES, TILE, HALF), BF),
        V((2, 8, HALF), F32),
        V((TILES, HD, TILE), BF),
        V((HALF, HD), BF),
        V((HD, HALF), F32),
        V((TILES, 2, TILE, HD), F32),
        V((TILES, 2, TILE, HD), F32),
        V((CHIPS, ROWS, HD), BF),
        V((CHIPS, ROWS, HD), BF),
        V((CHIPS, 2, ROWS, HD), BF),
        V((TILES, 3 * HD, TILE), BF),
        V((HEADS, 3, ROWS, HD), BF),
        V((3 * HD, CH), F32),
        V((12, 16, CH), BF),
        V((12, 16, CH), BF),
        V((24, 16, PART), BF),
        V((ZS, 3, 16, PART), BF),
        V((3, 16, PART), BF),
        V((3, 16, PART), BF),
        V((3, 16, PART), BF),
        V((ROWS + 2 * HALO, CH), BF),
        V((CHIPS, 96, ROWS), BF),
        V((CHIPS, 96, ROWS), BF),
        V((96, HALF), BF),
        V((2, TAPS * 96, PART), F32),
        V((2, 15, 16, PART), BF),
        V((2, 15, 16, PART), BF),
        V((16, 16, PART), BF),
        V((16, 16, PART), F32),
        V((ZS, 2, 16, PART), BF),
        V((ZS, 2, 16, PART), BF),
        V((ZS, 2, 16, PART), BF),
        sem(12),
        sem(3, 5), sem(3, 8), sem(3, 2, 2), sem(1), sem(1),
        sem(8), sem(8), sem(1), sem(1),
        sem(4), sem(4), sem(8), sem(8), sem(8), sem(8), sem(8), sem(8), sem(4), sem(4),
        sem(1), sem(1), sem(8), sem(8), sem(1), sem(1), sem(3, 8), sem(24),
        sem(2), sem(2), sem(8), sem(8), sem(2), sem(2),
        sem(8), sem(8), sem(8), sem(8), sem(16), sem(2, 8),
    ]
    att, gi, cfin, gfin = pl.pallas_call(
        kernel,
        out_shape=[
            jax.ShapeDtypeStruct((ROWS, INNER), BF),
            jax.ShapeDtypeStruct((ROWS, CH), BF),
            jax.ShapeDtypeStruct((2, 16, 16, PART), BF),
            jax.ShapeDtypeStruct((24, 16, PART), BF),
        ],
        in_specs=[hbm] * 5,
        out_specs=[vm, vm, vm, vm],
        scratch_shapes=scratch,
        compiler_params=pltpu.CompilerParams(
            collective_id=0, has_side_effects=True, vmem_limit_bytes=58 * 1024 * 1024
        ),
        cost_estimate=pl.CostEstimate(flops=14_000_000_000, bytes_accessed=15_000_000, transcendentals=3_000_000),
    )(inputs[0], gain, out_grad[0], convolution_weight, w_qkv)
    att, gi, conv, qkv = pl.pallas_call(
        finish,
        out_shape=[
            jax.ShapeDtypeStruct((ROWS, INNER), BF),
            jax.ShapeDtypeStruct((ROWS, CH), BF),
            jax.ShapeDtypeStruct((240, CH), F32),
            jax.ShapeDtypeStruct((192, CH), F32),
        ],
        in_specs=[vm, vm, vm, vm],
        out_specs=[hbm, hbm, hbm, hbm],
        scratch_shapes=[V((240, CH), F32), V((192, CH), F32), sem(4)],
    )(att, gi, cfin, gfin)
    return att[None], gi[None], conv.reshape(TAPS, 48, CH).transpose(0, 2, 1), qkv.T


def solution(mesh):
    in_specs = (P("dp", "seq", None), P(), P(), P(), P("dp", "seq", None))
    out_specs = (P("dp", "seq", None), P("dp", "seq", None), P(None, None, "seq"), P(None, "seq"))
    return jax.shard_map(body, mesh=mesh, in_specs=in_specs, out_specs=out_specs, check_vma=False)
```

time: 112 us -> 93.2 us (0.83)
  Pallas kernels: 105 us -> 92.3 us
  local copies, waits for them, and re-layouts: 6.43 us -> 0 us
    pallas_call x1, Pallas kernels: 102 us -> 89.8 us  [body(): pl.pallas_call(kernel, out_shape=[jax.ShapeDtypeStruct((ROWS, INNER), BF)...]
    unnamed x2 -> x0, local copies, waits for them, and re-layouts: 5.16 us -> none
    reshape x1 -> x0, local copies, waits for them, and re-layouts: 1.27 us -> none  [body(): gain.reshape(1, CH)]
where the time goes in v3:
time: 93.2 us; the launch traced here: 93.1 us
  Pallas kernels  92.3 us (99%)
    pallas_call x1, Pallas kernels, body(): pl.pallas_call(kernel, out_shape=[jax.ShapeDtypeStruct((ROWS, INNER), BF)...  89.8 us
    pallas_call x1, Pallas kernels, body(): pl.pallas_call(finish, out_shape=[jax.ShapeDtypeStruct((ROWS, INNER), BF)...  2.51 us

profile of v3, /device:TPU:1, one launch (start us, length us, event | category | flops | bytes accessed | tf_op | source)
XLA Modules:
  0.0 93.1 jit_solution(6675286005019088212)
XLA Ops:
  0.6 89.8 %shard_map.84 = (bf16[128,1024]{1,0:T(8,128)(2,1)}, bf16[128,768]{1,0:T(8,128)(2,1)}, bf16[2,16,16,384]{3,2,1,0:T(8,128)(2,1)}, bf16[24,16,384]{2,1,0:T(8,128)(2,1)}) custom-call(bf16[128,768]{1,0:T(8,128)(2,1)} %bitcast.12, f32[768]{0:T(1024)} %gain_hbm.1, bf16[128,1024]{1,0:T(8,128)(2,1)} %bitcast.10, bf16[5,768,768]{2,1,0:T(8,128)(2,1)} %cw_hbm.1, ...), custom_call_target="tpu_custom_call" | custom-call | flops 14000000000 | bytes 15000000 | tf_op jit(solution)/shard_map/pallas_call | solution.py:814
  90.4 2.5 %shard_map.85 = (bf16[128,1024]{1,0:T(8,128)(2,1)}, bf16[128,768]{1,0:T(8,128)(2,1)}, f32[240,768]{1,0:T(8,128)}, f32[192,768]{1,0:T(8,128)}) custom-call(bf16[128,1024]{1,0:T(8,128)(2,1)} %get-tuple-element.12.att_ref, bf16[128,768]{1,0:T(8,128)(2,1)} %get-tuple-element.13.gi_ref, bf16[2,16,16,384]{3,2,1,0:T(8,128)(2,1)} %get-tuple-element.14.cfin, ...), custom_call_target="tpu_custom_call" | custom-call | tf_op jit(solution)/shard_map/pallas_call | solution.py:830

commit v4 on v3

--- a/solution.py
+++ b/solution.py
@@ -66,13 +66,13 @@
 
 def kernel(
     x_hbm, gain_hbm, og_hbm, cw_hbm, w_hbm,
-    att_ref, gi_ref, cfin, gfin,
-    x_ref, gain_ref, og_ref, cwv, wfull, wh, xg, ag, apad, epad, acc_s, gn_s, hid_s, nh, doh, dot_s, qd, qt_s, kv, vt_s,
+    att_out, gi_out, ct_out, gq_out,
+    att_ref, gi_ref, cfin, gfin, ctf, gqf, x_ref, gain_ref, og_ref, cwv, wfull, wh, xg, ag, apad, epad, acc_s, gn_s, hid_s, nh, doh, dot_s, qd, qt_s, kv, vt_s,
     wts, stat_s, ot_s, dor_s, dqt, dkvp, pr, obuf, dqb, gsrc, gt, res, gtf, gst, grcv, gown,
     rq, redp, redr, red, bext, bst, bh, bt, cg, cst, crcv, give_c, keep_c, px, zs, rc,
     wsem, xs, xr, xps, xhs, xhr, dos, dor, hds, hdr, kvs, kvr, os_, or_, dqs, dqr, ks, kr, prs, prr,
     gps, gpr, rqs, rqr, rps, rpr, gus, gur, h2s, h2r, bs, br, cps, cpr,
-    pxs, pxr, rcs, rcr, fzs, fzr,
+    pxs, pxr, rcs, rcr, fzs, fzr, fxs, fxr,
 ):
     j = lax.axis_index("seq")
     d = lax.axis_index("dp")
@@ -374,19 +374,23 @@
             slope = (gw - stat_s[1, 0:1, lanes]) * stat_s[0, 0:1, lanes]
             parts.append((w[:, lanes].astype(F32) * slope).astype(BF))
         ds = jnp.concatenate(parts, axis=1)
-        dv = dot(w, dor_s[...])
-        dk = dot(ds, qd[...])
-        dqt[...] = dqt[...] + dot(kv[h, m, :, :HD].T, ds)
-        return dk * TEMPER, dv
+        return dot(ds, qd[...]) * TEMPER, dot(w, dor_s[...]), kv[h, m, :, :HD].T, ds
+
+    def add_queries(*parts):
+        keys = jnp.concatenate([part[2] for part in parts], axis=1)
+        dqt[...] = dqt[...] + dot(keys, jnp.concatenate([part[3] for part in parts], axis=0))
 
     def pr_copy(m):
         return rcopy(dkvp.at[m], pr.at[m], prs.at[m], prr.at[m], mate)
 
-    early = turn(0, 1 - k)
-    dk, dv = backward(1 - k, early)
-    dkvp[early, 0] = dk
-    dkvp[early, 1] = dv
-    pr_copy(early).start()
+    def hand_over(m, part):
+        dkvp[m, 0] = part[0]
+        dkvp[m, 1] = part[1]
+        pr_copy(m).start()
+
+    early = backward(1 - k, turn(0, 1 - k))
+    hand_over(turn(0, 1 - k), early)
+    add_queries(early)
 
     def kv_back(b):
         return rcopy(
@@ -396,21 +400,10 @@
     def kv_local(b):
         res[c, 1:3] = gsrc[b]
 
-    def halves(i):
-        m = turn(i, k)
-        ahead = turn(i + 1, 1 - k)
-
-        @pl.when(i < TILES - 1)
-        def _():
-            dk, dv = backward(1 - k, ahead)
-            dkvp[ahead, 0] = dk
-            dkvp[ahead, 1] = dv
-            pr_copy(ahead).start()
-
-        dk, dv = backward(k, m)
+    def complete(m, part):
         pr_copy(m).wait_recv()
-        dk = dk + pr[m, 0]
-        dv = dv + pr[m, 1]
+        dk = part[0] + pr[m, 0]
+        dv = part[1] + pr[m, 1]
         for e in range(2):
             gsrc[2 * m + e, 0] = dk[e * ROWS : (e + 1) * ROWS].astype(BF)
             gsrc[2 * m + e, 1] = dv[e * ROWS : (e + 1) * ROWS].astype(BF)
@@ -418,7 +411,17 @@
         gt[m, HD : 2 * HD, :] = dk.T.astype(BF)
         gt[m, 2 * HD :, :] = dv.T.astype(BF)
 
-    loop(TILES, halves)
+    def halves(i):
+        ahead = backward(1 - k, turn(i + 1, 1 - k))
+        own = backward(k, turn(i, k))
+        add_queries(ahead, own)
+        hand_over(turn(i + 1, 1 - k), ahead)
+        complete(turn(i, k), own)
+
+    loop(TILES - 1, halves)
+    last = backward(k, turn(TILES - 1, k))
+    add_queries(last)
+    complete(turn(TILES - 1, k), last)
 
     def dq_copy(b):
         return rcopy(
@@ -608,29 +611,46 @@
             else:
                 keep_c[t * 3 : t * 3 + 3] = both
 
-    def px_copy(off):
+    def px_copy(h, off):
         zz, _ = ring(off)
-        return rcopy(give_c.at[pl.ds(2 * zz, 2)], px.at[zz], pxs.at[zz], pxr.at[zz], partner)
+        return rcopy(give_c.at[2 * zz + h], px.at[h, zz], pxs.at[h, zz], pxr.at[h, zz], partner)
 
     with_mate(0)
-    for off in FAR + (0,):
-        px_copy(off).start()
+    for h in range(2):
+        for off in FAR + (0,):
+            px_copy(h, off).start()
     with_mate(1)
 
-    def rc_copy(off):
+    def rc_copy(h, off):
         zz, dev = ring(off)
-        return rcopy(zs.at[zz], rc.at[z], rcs.at[zz], rcr.at[z], dev)
-
-    for off in FAR + (0,):
-        zz, _ = ring(off)
-        px_copy(off).wait_recv()
-        both = (keep_c[pl.ds(2 * zz, 2)] + px[zz].astype(F32)).astype(BF)
-        if off:
-            zs[zz] = both
-            rc_copy(off).start()
-        else:
-            rc[z] = both
-
+        return rcopy(zs.at[h, zz], rc.at[h, z], rcs.at[h, zz], rcr.at[h, z], dev)
+
+    for h in range(2):
+        for off in FAR + (0,):
+            zz, _ = ring(off)
+            px_copy(h, off).wait_recv()
+            both = (keep_c[2 * zz + h] + px[h, zz].astype(F32)).astype(BF)
+            if off:
+                zs[h, zz] = both
+                rc_copy(h, off).start()
+            else:
+                rc[h, z] = both
+
+    def piece(n, h, zz):
+        return cfin.at[n, 2 * zz + h]
+
+    def fz_copy(h, off):
+        zz, dev = ring(off)
+        return rcopy(piece(xl, h, z), piece(xl, h, z), fzs.at[h, zz], fzr.at[h, z], dev)
+
+    def fx_copy(h, zz):
+        return rcopy(piece(xl, h, zz), piece(xl, h, zz), fxs.at[h, zz], fxr.at[h, zz], partner)
+
+    for h in range(2):
+        cfin[xl, 2 * z + h] = take(rc.at[h], rcs.at[h], rcr.at[h])
+        for off in FAR:
+            fz_copy(h, off).start()
+        fx_copy(h, z).start()
     edges.wait_recv()
     ga = jnp.zeros((ROWS, CH), F32)
     for t in range(TAPS):
@@ -641,16 +661,12 @@
     slope = 0.5 * (1.0 + th) + 0.5 * x * (1.0 - th * th) * GELU_A * (1.0 + 3.0 * GELU_B * x * x)
     gi_ref[...] = (hid_s[...] + slope * ga).astype(BF)
 
-    def pair(n, zz):
-        return cfin.at[n, pl.ds(2 * zz, 2)]
-
-    def fin_copy(i):
-        to = (d + i) % DP
-        return rcopy(pair(xl, z), pair(xl, z), fzs.at[to], fzr.at[xl, z], {"dp": to})
-
-    cfin[xl, pl.ds(2 * z, 2)] = take(rc, rcs, rcr)
-    for i in (8, 7, 9, 6, 10, 5, 11, 4, 12, 3, 13, 2, 14, 1, 15):
-        fin_copy(i).start()
+    for h in range(2):
+        for off in reversed(FAR):
+            zz, _ = ring(off)
+            here = piece(xl, h, zz)
+            rcopy(here, here, fzs.at[0, 0], fzr.at[h, zz], partner).wait_recv()
+            fx_copy(h, zz).start()
 
     def o_wait(chip):
         @pl.when(2 * chip + home != j)
@@ -659,6 +675,10 @@
             rcopy(obuf.at[0], att_ref.at[:, lanes], os_.at[0], or_.at[chip], mate).wait_recv()
 
     loop(CHIPS, o_wait)
+    att_copy = pltpu.make_async_copy(att_ref, att_out, wsem.at[12])
+    gi_copy = pltpu.make_async_copy(gi_ref, gi_out, wsem.at[13])
+    att_copy.start()
+    gi_copy.start()
 
     def land_q(row):
         u = 3 * j + row // 8
@@ -669,15 +689,21 @@
             rcopy(red.at[0], gfin.at[row], gus.at[0, 0], gur.at[row], mate).wait_recv()
 
     loop(24, land_q)
+    for r in range(3):
+        for h in range(2):
+            block = gfin[8 * r + 4 * h : 8 * r + 4 * h + 4].astype(F32).reshape(64, PART)
+            gqf[64 * r : 64 * r + 64, h * PART : (h + 1) * PART] = block
+    gq_copy = pltpu.make_async_copy(gqf, gq_out, wsem.at[14])
+    gq_copy.start()
     def land_c(i):
-        n = i // ZS
-        zz = i % ZS
-
-        @pl.when((n != xl) | (zz != z))
-        def _():
-            rcopy(pair(n, zz), pair(n, zz), fzs.at[0], fzr.at[n, zz], partner).wait_recv()
-
-    loop(DP, land_c)
+        here = piece(1 - xl, i // ZS, i % ZS)
+        rcopy(here, here, fzs.at[0, 0], fxr.at[i // ZS, i % ZS], partner).wait_recv()
+
+    loop(2 * ZS, land_c)
+    for n in range(2):
+        ctf[:, n * PART : (n + 1) * PART] = cfin[n, :15].astype(F32).reshape(240, PART)
+    ct_copy = pltpu.make_async_copy(ctf, ct_out, wsem.at[15])
+    ct_copy.start()
 
     for g in range(GROUPS):
         if g == GROUPS - 1:
@@ -718,32 +744,34 @@
         cp_copy(o).wait_send()
     for off in FAR:
         rq_copy(off).wait_send()
-        rc_copy(off).wait_send()
+        rc_copy(0, off).wait_send()
+        rc_copy(1, off).wait_send()
     for off in range(ZS):
-        px_copy(off).wait_send()
-    loop(15, lambda i: fin_copy(i + 1).wait_send())
-
-
-def finish(att_ref, gi_ref, cfin, gfin, att_out, gi_out, cw_out, w_out, cbuf, gbuf, sem):
-    copies = [pltpu.make_async_copy(att_ref, att_out, sem.at[0]), pltpu.make_async_copy(gi_ref, gi_out, sem.at[1])]
-    for cp in copies:
-        cp.start()
-    for r in range(3):
+        px_copy(0, off).wait_send()
+        px_copy(1, off).wait_send()
         for h in range(2):
-            piece = gfin[8 * r + 4 * h : 8 * r + 4 * h + 4].astype(F32).reshape(64, PART)
-            gbuf[64 * r : 64 * r + 64, h * PART : (h + 1) * PART] = piece
-    copies.append(pltpu.make_async_copy(gbuf, w_out, sem.at[2]))
-    copies[-1].start()
-    for n in range(2):
-        cbuf[:, n * PART : (n + 1) * PART] = cfin[n, :15].astype(F32).reshape(240, PART)
-    copies.append(pltpu.make_async_copy(cbuf, cw_out, sem.at[3]))
-    copies[-1].start()
-    for cp in copies:
-        cp.wait()
+            fx_copy(h, ring(off)[0]).wait_send()
+            if off:
+                fz_copy(h, off).wait_send()
+
+    for copy in (att_copy, gi_copy, gq_copy, ct_copy):
+        copy.wait()
+
+
+def finish(a, b, c, d, a_out, b_out, c_out, d_out, a_buf, b_buf, c_buf, d_buf, sem):
+    parts = ((a, a_buf, a_out), (b, b_buf, b_out), (c, c_buf, c_out), (d, d_buf, d_out))
+    reads = [pltpu.make_async_copy(src, buf, sem.at[i]) for i, (src, buf, _) in enumerate(parts)]
+    writes = [pltpu.make_async_copy(buf, dst, sem.at[4 + i]) for i, (_, buf, dst) in enumerate(parts)]
+    for copy in reads:
+        copy.start()
+    for i in range(4):
+        reads[i].wait()
+        writes[i].start()
+    for copy in writes:
+        copy.wait()
 
 
 def body(inputs, convolution_weight, w_qkv, gain, out_grad):
-    vm = pl.BlockSpec(memory_space=pltpu.VMEM)
     hbm = pl.BlockSpec(memory_space=pl.ANY)
     V = pltpu.VMEM
 
@@ -751,6 +779,12 @@
         return pltpu.SemaphoreType.DMA(n)
 
     scratch = [
+        V((ROWS, INNER), BF),
+        V((ROWS, CH), BF),
+        V((2, 16, 16, PART), BF),
+        V((24, 16, PART), BF),
+        V((240, CH), F32),
+        V((192, CH), F32),
         V((ROWS, CH), BF),
         V((CH,), F32),
         V((ROWS, INNER), BF),
@@ -800,27 +834,28 @@
         V((2, 15, 16, PART), BF),
         V((16, 16, PART), BF),
         V((16, 16, PART), F32),
-        V((ZS, 2, 16, PART), BF),
-        V((ZS, 2, 16, PART), BF),
-        V((ZS, 2, 16, PART), BF),
-        sem(12),
+        V((2, ZS, 16, PART), BF),
+        V((2, ZS, 16, PART), BF),
+        V((2, ZS, 16, PART), BF),
+        sem(16),
         sem(3, 5), sem(3, 8), sem(3, 2, 2), sem(1), sem(1),
         sem(8), sem(8), sem(1), sem(1),
         sem(4), sem(4), sem(8), sem(8), sem(8), sem(8), sem(8), sem(8), sem(4), sem(4),
         sem(1), sem(1), sem(8), sem(8), sem(1), sem(1), sem(3, 8), sem(24),
         sem(2), sem(2), sem(8), sem(8), sem(2), sem(2),
-        sem(8), sem(8), sem(8), sem(8), sem(16), sem(2, 8),
+        sem(2, 8), sem(2, 8), sem(2, 8), sem(2, 8), sem(2, 8), sem(2, 8),
+        sem(2, 8), sem(2, 8),
     ]
     att, gi, cfin, gfin = pl.pallas_call(
         kernel,
         out_shape=[
             jax.ShapeDtypeStruct((ROWS, INNER), BF),
             jax.ShapeDtypeStruct((ROWS, CH), BF),
-            jax.ShapeDtypeStruct((2, 16, 16, PART), BF),
-            jax.ShapeDtypeStruct((24, 16, PART), BF),
+            jax.ShapeDtypeStruct((240, CH), F32),
+            jax.ShapeDtypeStruct((192, CH), F32),
         ],
         in_specs=[hbm] * 5,
-        out_specs=[vm, vm, vm, vm],
+        out_specs=[hbm] * 4,
         scratch_shapes=scratch,
         compiler_params=pltpu.CompilerParams(
             collective_id=0, has_side_effects=True, vmem_limit_bytes=58 * 1024 * 1024
@@ -835,9 +870,9 @@
             jax.ShapeDtypeStruct((240, CH), F32),
             jax.ShapeDtypeStruct((192, CH), F32),
         ],
-        in_specs=[vm, vm, vm, vm],
-        out_specs=[hbm, hbm, hbm, hbm],
-        scratch_shapes=[V((240, CH), F32), V((192, CH), F32), sem(4)],
+        in_specs=[hbm] * 4,
+        out_specs=[hbm] * 4,
+        scratch_shapes=[V((ROWS, INNER), BF), V((ROWS, CH), BF), V((240, CH), F32), V((192, CH), F32), sem(8)],
     )(att, gi, cfin, gfin)
     return att[None], gi[None], conv.reshape(TAPS, 48, CH).transpose(0, 2, 1), qkv.T
 

time: 93.2 us -> 89.1 us (0.956)
  Pallas kernels: 92.3 us -> 87.5 us
    pallas_call x1, Pallas kernels: 89.8 us -> 85.1 us  [body(): pl.pallas_call(kernel, out_shape=[jax.ShapeDtypeStruct((ROWS, INNER), BF)...]
where the time goes in v4:
time: 89.1 us; the launch traced here: 88.3 us
  Pallas kernels  87.5 us (98%)
    pallas_call x1, Pallas kernels, body(): pl.pallas_call(kernel, out_shape=[jax.ShapeDtypeStruct((ROWS, INNER), BF)...  85.1 us
    pallas_call x1, Pallas kernels, body(): pl.pallas_call(finish, out_shape=[jax.ShapeDtypeStruct((ROWS, INNER), BF)...  2.42 us

profile of v4, /device:TPU:1, one launch (start us, length us, event | category | flops | bytes accessed | tf_op | source)
XLA Modules:
  0.0 88.3 jit_solution(11555662166458499994)
XLA Ops:
  0.6 85.1 %shard_map.84 = (bf16[128,1024]{1,0:T(8,128)(2,1)}, bf16[128,768]{1,0:T(8,128)(2,1)}, f32[240,768]{1,0:T(8,128)}, f32[192,768]{1,0:T(8,128)}) custom-call(bf16[128,768]{1,0:T(8,128)(2,1)} %bitcast.12, f32[768]{0:T(1024)} %gain_hbm.1, bf16[128,1024]{1,0:T(8,128)(2,1)} %bitcast.10, bf16[5,768,768]{2,1,0:T(8,128)(2,1)} %cw_hbm.1, bf16[768,3072]{1,0:T(8,128)(2,1)} %w_hbm.1), custom_call_target="tpu_custom_call" | custom-call | flops 14000000000 | bytes 15000000 | tf_op jit(solution)/shard_map/pallas_call | solution.py:849
  85.7 2.4 %shard_map.85 = (bf16[128,1024]{1,0:T(8,128)(2,1)}, bf16[128,768]{1,0:T(8,128)(2,1)}, f32[240,768]{1,0:T(8,128)}, f32[192,768]{1,0:T(8,128)}) custom-call(bf16[128,1024]{1,0:T(8,128)(2,1)} %get-tuple-element.12.a, bf16[128,768]{1,0:T(8,128)(2,1)} %get-tuple-element.13.b, f32[240,768]{1,0:T(8,128)} %get-tuple-element.14.c, f32[192,768]{1,0:T(8,128)} %get-tuple-element.15.d), custom_call_target="tpu_custom_call" | custom-call | tf_op jit(solution)/shard_map/pallas_call | solution.py:865

commit v5 on v4

--- a/solution.py
+++ b/solution.py
@@ -172,7 +172,6 @@
 
     x_in.wait()
     send_x(0)
-    x_left(0)
     send_x(1)
 
     inside = c // 4 == k
@@ -243,9 +242,8 @@
     for t in range(TAPS):
         pltpu.make_async_copy(cw_hbm.at[t], cwv.at[t], wsem.at[t]).wait()
     relay(0)
+    send_x(2)
     unit(0, True)
-    x_left(1)
-    send_x(2)
     relay(1)
     unit(1, True)
     unit(0, False)
@@ -699,15 +697,19 @@
         here = piece(1 - xl, i // ZS, i % ZS)
         rcopy(here, here, fzs.at[0, 0], fxr.at[i // ZS, i % ZS], partner).wait_recv()
 
+    def write_taps(n):
+        ctf[n] = cfin[n, :15].astype(F32).reshape(240, PART)
+        lanes = pl.ds(pl.multiple_of(n * PART, PART), PART)
+        copy = pltpu.make_async_copy(ctf.at[n], ct_out.at[:, lanes], wsem.at[15 + n])
+        copy.start()
+        return copy
+
+    ct_own = write_taps(xl)
     loop(2 * ZS, land_c)
-    for n in range(2):
-        ctf[:, n * PART : (n + 1) * PART] = cfin[n, :15].astype(F32).reshape(240, PART)
-    ct_copy = pltpu.make_async_copy(ctf, ct_out, wsem.at[15])
-    ct_copy.start()
+    ct_other = write_taps(1 - xl)
 
     for g in range(GROUPS):
-        if g == GROUPS - 1:
-            x_left(g)
+        x_left(g)
         pl.when(home != k)(lambda g=g: x_copy(g, 4).wait_send())
         for e in range(2):
             pass_copy(g, e, flip_x, 0).wait_send()
@@ -754,7 +756,7 @@
             if off:
                 fz_copy(h, off).wait_send()
 
-    for copy in (att_copy, gi_copy, gq_copy, ct_copy):
+    for copy in (att_copy, gi_copy, gq_copy, ct_own, ct_other):
         copy.wait()
 
 
@@ -783,7 +785,7 @@
         V((ROWS, CH), BF),
         V((2, 16, 16, PART), BF),
         V((24, 16, PART), BF),
-        V((240, CH), F32),
+        V((2, 240, PART), F32),
         V((192, CH), F32),
         V((ROWS, CH), BF),
         V((CH,), F32),
@@ -837,7 +839,7 @@
         V((2, ZS, 16, PART), BF),
         V((2, ZS, 16, PART), BF),
         V((2, ZS, 16, PART), BF),
-        sem(16),
+        sem(17),
         sem(3, 5), sem(3, 8), sem(3, 2, 2), sem(1), sem(1),
         sem(8), sem(8), sem(1), sem(1),
         sem(4), sem(4), sem(8), sem(8), sem(8), sem(8), sem(8), sem(8), sem(4), sem(4),

time: 89.1 us -> 88.8 us (level)
  no operation moved by 1% of the time
where the time goes in v5:
time: 88.8 us; the launch traced here: 88.2 us
  Pallas kernels  87.4 us (98%)
    pallas_call x1, Pallas kernels, body(): pl.pallas_call(kernel, out_shape=[jax.ShapeDtypeStruct((ROWS, INNER), BF)...  85 us
    pallas_call x1, Pallas kernels, body(): pl.pallas_call(finish, out_shape=[jax.ShapeDtypeStruct((ROWS, INNER), BF)...  2.42 us

profile of v5, /device:TPU:1, one launch (start us, length us, event | category | flops | bytes accessed | tf_op | source)
XLA Modules:
  0.0 88.2 jit_solution(12459092030773145410)
XLA Ops:
  0.6 85.0 %shard_map.84 = (bf16[128,1024]{1,0:T(8,128)(2,1)}, bf16[128,768]{1,0:T(8,128)(2,1)}, f32[240,768]{1,0:T(8,128)}, f32[192,768]{1,0:T(8,128)}) custom-call(bf16[128,768]{1,0:T(8,128)(2,1)} %bitcast.12, f32[768]{0:T(1024)} %gain_hbm.1, bf16[128,1024]{1,0:T(8,128)(2,1)} %bitcast.10, bf16[5,768,768]{2,1,0:T(8,128)(2,1)} %cw_hbm.1, bf16[768,3072]{1,0:T(8,128)(2,1)} %w_hbm.1), custom_call_target="tpu_custom_call" | custom-call | flops 14000000000 | bytes 15000000 | tf_op jit(solution)/shard_map/pallas_call | solution.py:851
  85.6 2.4 %shard_map.85 = (bf16[128,1024]{1,0:T(8,128)(2,1)}, bf16[128,768]{1,0:T(8,128)(2,1)}, f32[240,768]{1,0:T(8,128)}, f32[192,768]{1,0:T(8,128)}) custom-call(bf16[128,1024]{1,0:T(8,128)(2,1)} %get-tuple-element.12.a, bf16[128,768]{1,0:T(8,128)(2,1)} %get-tuple-element.13.b, f32[240,768]{1,0:T(8,128)} %get-tuple-element.14.c, f32[192,768]{1,0:T(8,128)} %get-tuple-element.15.d), custom_call_target="tpu_custom_call" | custom-call | tf_op jit(solution)/shard_map/pallas_call | solution.py:867

commit v6 on v5

--- a/solution.py
+++ b/solution.py
@@ -172,6 +172,7 @@
 
     x_in.wait()
     send_x(0)
+    x_left(0)
     send_x(1)
 
     inside = c // 4 == k
@@ -242,8 +243,9 @@
     for t in range(TAPS):
         pltpu.make_async_copy(cw_hbm.at[t], cwv.at[t], wsem.at[t]).wait()
     relay(0)
+    unit(0, True)
+    x_left(1)
     send_x(2)
-    unit(0, True)
     relay(1)
     unit(1, True)
     unit(0, False)
@@ -709,7 +711,8 @@
     ct_other = write_taps(1 - xl)
 
     for g in range(GROUPS):
-        x_left(g)
+        if g == GROUPS - 1:
+            x_left(g)
         pl.when(home != k)(lambda g=g: x_copy(g, 4).wait_send())
         for e in range(2):
             pass_copy(g, e, flip_x, 0).wait_send()

time: 88.8 us -> 89 us (level)
  no operation moved by 1% of the time
where the time goes in v6:
time: 89 us; the launch traced here: 88.2 us
  Pallas kernels  87.4 us (98%)
    pallas_call x1, Pallas kernels, body(): pl.pallas_call(kernel, out_shape=[jax.ShapeDtypeStruct((ROWS, INNER), BF)...  85 us
    pallas_call x1, Pallas kernels, body(): pl.pallas_call(finish, out_shape=[jax.ShapeDtypeStruct((ROWS, INNER), BF)...  2.42 us

profile of v6, /device:TPU:1, one launch (start us, length us, event | category | flops | bytes accessed | tf_op | source)
XLA Modules:
  0.0 88.2 jit_solution(926078817773001298)
XLA Ops:
  0.6 85.0 %shard_map.84 = (bf16[128,1024]{1,0:T(8,128)(2,1)}, bf16[128,768]{1,0:T(8,128)(2,1)}, f32[240,768]{1,0:T(8,128)}, f32[192,768]{1,0:T(8,128)}) custom-call(bf16[128,768]{1,0:T(8,128)(2,1)} %bitcast.12, f32[768]{0:T(1024)} %gain_hbm.1, bf16[128,1024]{1,0:T(8,128)(2,1)} %bitcast.10, bf16[5,768,768]{2,1,0:T(8,128)(2,1)} %cw_hbm.1, bf16[768,3072]{1,0:T(8,128)(2,1)} %w_hbm.1), custom_call_target="tpu_custom_call" | custom-call | flops 14000000000 | bytes 15000000 | tf_op jit(solution)/shard_map/pallas_call | solution.py:854
  85.6 2.4 %shard_map.85 = (bf16[128,1024]{1,0:T(8,128)(2,1)}, bf16[128,768]{1,0:T(8,128)(2,1)}, f32[240,768]{1,0:T(8,128)}, f32[192,768]{1,0:T(8,128)}) custom-call(bf16[128,1024]{1,0:T(8,128)(2,1)} %get-tuple-element.12.a, bf16[128,768]{1,0:T(8,128)(2,1)} %get-tuple-element.13.b, f32[240,768]{1,0:T(8,128)} %get-tuple-element.14.c, f32[192,768]{1,0:T(8,128)} %get-tuple-element.15.d), custom_call_target="tpu_custom_call" | custom-call | tf_op jit(solution)/shard_map/pallas_call | solution.py:870
